TPU v7x, 128 devices: a whole 4x4x4 slice. The times are simulated.
128 devices in a mesh: tm: 32 (over z, x, core), space: 4 (over y).
Axes of the slice: x: 4, y: 4, z: 4, core: 2. Of those that a mesh axis runs over, the one named last changes fastest.
Arguments:
- latents: bfloat16 [256, 256, 1536], P('tm', 'space'), may hold values from -6 to 6
- mixer_weight: bfloat16 [1536, 1792], replicated, may hold values from -0.15625 to 0.15625
- step_weight: bfloat16 [1536, 12], replicated, may hold values from -0.15625 to 0.15625
- step_bias: float32 [12], replicated, may hold values from -1 to 0.5
- decay_rate: float32 [12], replicated, may hold values from 6.1035156e-06 to 0.06, as said below
- attend_weight: bfloat16 [1536, 2304], replicated, may hold values from -0.15625 to 0.15625
- output_weight: bfloat16 [2304, 1536], replicated, may hold values from -0.125 to 0.125
Outputs:
- updated: bfloat16 [256, 256, 1536], P('tm', 'space')
Inputs may be any that keep to these rules, and one draw needn't show every extreme that they name: `decay_rate`: decay rates of the heads' states.
All inputs are finite; a program needn't handle non-finite values.
Results may differ from a plain program's by a relative error of at most 0.009.
Values may be sent and summed in bfloat16 or wider, within the bound.
A program may use at most 192 MiB of HBM per device.

v0:
```python
import math

import jax
import jax.numpy as jnp
from jax import lax
from jax.sharding import PartitionSpec as P


def shifted(value, axis, steps):
    count = lax.axis_size(axis)
    leading, last = (max(0, -steps), min(count, count - steps))
    return lax.ppermute(value, axis, [(source, source + steps) for source in range(leading, last)])


def qk_scale(values):
    return values * lax.rsqrt(jnp.mean(values * values, axis=-1, keepdims=True) + 1e-06)


def local_states(inputs_u, b_proj, c_proj, dt_step, decay_rate):
    span_len = dt_step.shape[0]
    log_decay = jnp.cumsum(-decay_rate[None, :] * dt_step, axis=0)
    pair_dot = jnp.dot(c_proj, b_proj.T, preferred_element_type=jnp.float32)
    log_gap = log_decay.T[:, :, None] - log_decay.T[:, None, :]
    positions = jnp.arange(span_len)
    causal = positions[:, None] >= positions[None, :]
    weights = (
        jnp.where(causal, jnp.exp(jnp.where(causal, log_gap, 0.0)), 0.0)
        * pair_dot[None]
        * dt_step.T[:, None, :]
    )
    weights = weights.astype(jnp.bfloat16)
    local_y = jnp.einsum("hts,shp->thp", weights, inputs_u, preferred_element_type=jnp.float32)
    span_end = log_decay[-1]
    scaled = ((jnp.exp(span_end[None, :] - log_decay) * dt_step)[:, :, None] * inputs_u).astype(
        jnp.bfloat16
    )
    local_state = jnp.einsum("shp,sn->hpn", scaled, b_proj, preferred_element_type=jnp.float32)
    return (local_y, local_state, jnp.exp(span_end), log_decay)


def on_device(
    latents, mixer_weight, step_weight, step_bias, decay_rate, attend_weight, output_weight
):
    frame_count, block_len, model_width = latents.shape
    row_count = frame_count * block_len
    head_count = step_bias.shape[0]
    head_dim = model_width // head_count
    state_dim = (mixer_weight.shape[1] - model_width) // 2
    attend_width = attend_weight.shape[1] // 3
    attend_heads = attend_width // head_dim
    wide_in = latents.reshape(row_count, model_width).astype(jnp.float32)
    normed = (
        wide_in * lax.rsqrt(jnp.mean(wide_in * wide_in, axis=-1, keepdims=True) + 1e-06)
    ).astype(jnp.bfloat16)
    projected = jnp.dot(normed, mixer_weight, preferred_element_type=jnp.float32)
    inputs_u = (
        projected[:, :model_width].astype(jnp.bfloat16).reshape(row_count, head_count, head_dim)
    )
    b_proj = projected[:, model_width : model_width + state_dim].astype(jnp.bfloat16)
    c_proj = projected[:, model_width + state_dim :].astype(jnp.bfloat16)
    dt_step = jax.nn.softplus(
        jnp.dot(normed, step_weight, preferred_element_type=jnp.float32) + step_bias
    )
    local_y, local_state, total_decay, log_decay = local_states(
        inputs_u, b_proj, c_proj, dt_step, decay_rate
    )

    def advance(counter, carry_in):
        return shifted(total_decay[:, None, None] * carry_in + local_state, "tm", 1)

    incoming = lax.fori_loop(0, lax.axis_size("tm") - 1, advance, jnp.zeros_like(local_state))
    carried = jnp.exp(log_decay)[:, :, None] * jnp.einsum(
        "tn,hpn->thp", c_proj.astype(jnp.float32), incoming, precision=lax.Precision.HIGHEST
    )
    mixed_y = local_y + carried
    ssm_out = (
        (mixed_y * lax.rsqrt(jnp.mean(mixed_y * mixed_y, axis=-1, keepdims=True) + 1e-05))
        .astype(jnp.bfloat16)
        .reshape(row_count, model_width)
    )
    attend = jnp.dot(normed, attend_weight, preferred_element_type=jnp.float32).reshape(
        row_count, 3, attend_heads, head_dim
    )
    queries = (
        qk_scale(attend[:, 0])
        .astype(jnp.bfloat16)
        .reshape(frame_count, block_len, attend_heads, head_dim)
    )
    keys_now = qk_scale(attend[:, 1]).astype(jnp.bfloat16).reshape(row_count, attend_width)
    values_now = attend[:, 2].astype(jnp.bfloat16).reshape(row_count, attend_width)
    key_value = jnp.concatenate([keys_now, values_now], axis=-1).reshape(
        frame_count, block_len, 2 * attend_width
    )
    earlier_frame = shifted(key_value[-1], "tm", 1)
    key_frames = jnp.concatenate([earlier_frame[None], key_value[:-1]], axis=0)
    score_scale = 1.0 / math.sqrt(head_dim)
    portion = lax.all_gather(key_frames, "space", axis=1, tiled=True)
    key_count = portion.shape[1]
    part_keys = portion[:, :, :attend_width].reshape(frame_count, key_count, attend_heads, head_dim)
    part_values = portion[:, :, attend_width:].reshape(
        frame_count, key_count, attend_heads, head_dim
    )
    scores = (
        jnp.einsum("fqhd,fkhd->fhqk", queries, part_keys, preferred_element_type=jnp.float32)
        * score_scale
    )
    powers = jnp.exp(scores)
    numerator = jnp.einsum(
        "fhqk,fkhd->fqhd",
        powers.astype(jnp.bfloat16),
        part_values,
        preferred_element_type=jnp.float32,
    )
    numerator, denominator = (numerator, jnp.sum(powers, axis=-1))
    frame_ids = lax.axis_index("tm") * frame_count + jnp.arange(frame_count)
    present = (frame_ids > 0).astype(jnp.float32)
    attended = (
        (
            numerator
            / jnp.transpose(denominator, (0, 2, 1))[..., None]
            * present[:, None, None, None]
        )
        .astype(jnp.bfloat16)
        .reshape(row_count, attend_width)
    )
    result = (
        wide_in
        + jnp.dot(ssm_out, output_weight[:model_width], preferred_element_type=jnp.float32)
        + jnp.dot(attended, output_weight[model_width:], preferred_element_type=jnp.float32)
    )
    return result.astype(jnp.bfloat16).reshape(frame_count, block_len, model_width)


def solution(mesh):
    in_specs = (P("tm", "space", None), P(), P(), P(), P(), P(), P())
    out_specs = P("tm", "space", None)
    return jax.shard_map(
        on_device, mesh=mesh, in_specs=in_specs, out_specs=out_specs, check_vma=False
    )
```

profile of v0, /device:TPU:32, one launch (start us, length us, event | category | flops | bytes accessed | tf_op | source)
XLA Modules:
  0.0 579.4 jit_solution(1977994960575473448)
XLA Ops:
  10.1 10.3 %copy.32 = bf16[1536,2304]{0,1:T(8,128)(2,1)} copy(bf16[1536,2304]{1,0:T(8,128)(2,1)} %param.14) | data formatting | bytes 14155776 | tf_op args[5]
  20.4 6.1 %fusion.47 = f32[512,3,6,128]{0,3,2,1:T(8,128)S(1)} fusion(bf16[512,1536,1,1]{1,0,3,2:T(8,128)(2,1)S(1)} %bitcast.96, bf16[3,6,128,1536]{3,2,1,0:T(8,128)(2,1)} %bitcast.88), kind=kOutput, calls=%fused_computation.79 | convolution fusion | flops 3623878656 | bytes 13369344 | tf_op jit(solution)/shard_map/dot_general | solution.py:81
  36.1 5.6 convolution_convert_fusion
  48.0 2.1 fusion.19
  53.9 482.5 %while.10 = (s32[]{:T(128)}, f32[12,128,128]{2,1,0:T(8,128)S(1)}, f32[12]{0:T(128)S(1)}, f32[12,128,128]{2,1,0:T(8,128)S(1)}, s32[]{:T(128)}) while((s32[]{:T(128)}, f32[12,128,128]{2,1,0:T(8,128)S(1)}, f32[12]{0:T(128)S(1)}, f32[12,128,128]{2,1,0:T(8,128)S(1)}, s32[]{:T(128)}) %tuple.27), condition=%wide.region_4.5_spmd, body=%wide.region_3.4_spmd.sunk | while | flops 393218 | bytes 5505173 | solution.py:71
  54.0 3.5 collective-permute-start
  57.6 11.9 %collective-permute-done = f32[12,128,128]{2,1,0:T(8,128)S(1)} collective-permute-done((f32[12,128,128]{2,1,0:T(8,128)S(1)}, f32[12,128,128]{2,1,0:T(8,128)S(1)}, u32[]{:S(2)}, u32[]{:S(2)}) %collective-permute-start) | collective-permute-done | bytes 786464 | tf_op jit(solution)/shard_map/while/body/eval_jaxpr/ppermute | solution.py:12
  71.5 13.5 %collective-permute-done = f32[12,128,128]{2,1,0:T(8,128)S(1)} collective-permute-done((f32[12,128,128]{2,1,0:T(8,128)S(1)}, f32[12,128,128]{2,1,0:T(8,128)S(1)}, u32[]{:S(2)}, u32[]{:S(2)}) %collective-permute-start) | collective-permute-done | bytes 786464 | tf_op jit(solution)/shard_map/while/body/eval_jaxpr/ppermute | solution.py:12
  85.2 1.9 collective-permute-start
  87.1 13.5 %collective-permute-done = f32[12,128,128]{2,1,0:T(8,128)S(1)} collective-permute-done((f32[12,128,128]{2,1,0:T(8,128)S(1)}, f32[12,128,128]{2,1,0:T(8,128)S(1)}, u32[]{:S(2)}, u32[]{:S(2)}) %collective-permute-start) | collective-permute-done | bytes 786464 | tf_op jit(solution)/shard_map/while/body/eval_jaxpr/ppermute | solution.py:12
  100.7 1.9 collective-permute-start
  102.7 13.5 %collective-permute-done = f32[12,128,128]{2,1,0:T(8,128)S(1)} collective-permute-done((f32[12,128,128]{2,1,0:T(8,128)S(1)}, f32[12,128,128]{2,1,0:T(8,128)S(1)}, u32[]{:S(2)}, u32[]{:S(2)}) %collective-permute-start) | collective-permute-done | bytes 786464 | tf_op jit(solution)/shard_map/while/body/eval_jaxpr/ppermute | solution.py:12
  118.2 13.5 %collective-permute-done = f32[12,128,128]{2,1,0:T(8,128)S(1)} collective-permute-done((f32[12,128,128]{2,1,0:T(8,128)S(1)}, f32[12,128,128]{2,1,0:T(8,128)S(1)}, u32[]{:S(2)}, u32[]{:S(2)}) %collective-permute-start) | collective-permute-done | bytes 786464 | tf_op jit(solution)/shard_map/while/body/eval_jaxpr/ppermute | solution.py:12
  133.8 13.5 %collective-permute-done = f32[12,128,128]{2,1,0:T(8,128)S(1)} collective-permute-done((f32[12,128,128]{2,1,0:T(8,128)S(1)}, f32[12,128,128]{2,1,0:T(8,128)S(1)}, u32[]{:S(2)}, u32[]{:S(2)}) %collective-permute-start) | collective-permute-done | bytes 786464 | tf_op jit(solution)/shard_map/while/body/eval_jaxpr/ppermute | solution.py:12
  149.4 13.5 %collective-permute-done = f32[12,128,128]{2,1,0:T(8,128)S(1)} collective-permute-done((f32[12,128,128]{2,1,0:T(8,128)S(1)}, f32[12,128,128]{2,1,0:T(8,128)S(1)}, u32[]{:S(2)}, u32[]{:S(2)}) %collective-permute-start) | collective-permute-done | bytes 786464 | tf_op jit(solution)/shard_map/while/body/eval_jaxpr/ppermute | solution.py:12
  164.9 13.5 %collective-permute-done = f32[12,128,128]{2,1,0:T(8,128)S(1)} collective-permute-done((f32[12,128,128]{2,1,0:T(8,128)S(1)}, f32[12,128,128]{2,1,0:T(8,128)S(1)}, u32[]{:S(2)}, u32[]{:S(2)}) %collective-permute-start) | collective-permute-done | bytes 786464 | tf_op jit(solution)/shard_map/while/body/eval_jaxpr/ppermute | solution.py:12
  178.6 1.9 collective-permute-start
  180.5 13.5 %collective-permute-done = f32[12,128,128]{2,1,0:T(8,128)S(1)} collective-permute-done((f32[12,128,128]{2,1,0:T(8,128)S(1)}, f32[12,128,128]{2,1,0:T(8,128)S(1)}, u32[]{:S(2)}, u32[]{:S(2)}) %collective-permute-start) | collective-permute-done | bytes 786464 | tf_op jit(solution)/shard_map/while/body/eval_jaxpr/ppermute | solution.py:12
  196.1 13.5 %collective-permute-done = f32[12,128,128]{2,1,0:T(8,128)S(1)} collective-permute-done((f32[12,128,128]{2,1,0:T(8,128)S(1)}, f32[12,128,128]{2,1,0:T(8,128)S(1)}, u32[]{:S(2)}, u32[]{:S(2)}) %collective-permute-start) | collective-permute-done | bytes 786464 | tf_op jit(solution)/shard_map/while/body/eval_jaxpr/ppermute | solution.py:12
  211.6 13.5 %collective-permute-done = f32[12,128,128]{2,1,0:T(8,128)S(1)} collective-permute-done((f32[12,128,128]{2,1,0:T(8,128)S(1)}, f32[12,128,128]{2,1,0:T(8,128)S(1)}, u32[]{:S(2)}, u32[]{:S(2)}) %collective-permute-start) | collective-permute-done | bytes 786464 | tf_op jit(solution)/shard_map/while/body/eval_jaxpr/ppermute | solution.py:12
  227.2 13.5 %collective-permute-done = f32[12,128,128]{2,1,0:T(8,128)S(1)} collective-permute-done((f32[12,128,128]{2,1,0:T(8,128)S(1)}, f32[12,128,128]{2,1,0:T(8,128)S(1)}, u32[]{:S(2)}, u32[]{:S(2)}) %collective-permute-start) | collective-permute-done | bytes 786464 | tf_op jit(solution)/shard_map/while/body/eval_jaxpr/ppermute | solution.py:12
  242.8 13.5 %collective-permute-done = f32[12,128,128]{2,1,0:T(8,128)S(1)} collective-permute-done((f32[12,128,128]{2,1,0:T(8,128)S(1)}, f32[12,128,128]{2,1,0:T(8,128)S(1)}, u32[]{:S(2)}, u32[]{:S(2)}) %collective-permute-start) | collective-permute-done | bytes 786464 | tf_op jit(solution)/shard_map/while/body/eval_jaxpr/ppermute | solution.py:12
  258.3 13.5 %collective-permute-done = f32[12,128,128]{2,1,0:T(8,128)S(1)} collective-permute-done((f32[12,128,128]{2,1,0:T(8,128)S(1)}, f32[12,128,128]{2,1,0:T(8,128)S(1)}, u32[]{:S(2)}, u32[]{:S(2)}) %collective-permute-start) | collective-permute-done | bytes 786464 | tf_op jit(solution)/shard_map/while/body/eval_jaxpr/ppermute | solution.py:12
  273.9 13.5 %collective-permute-done = f32[12,128,128]{2,1,0:T(8,128)S(1)} collective-permute-done((f32[12,128,128]{2,1,0:T(8,128)S(1)}, f32[12,128,128]{2,1,0:T(8,128)S(1)}, u32[]{:S(2)}, u32[]{:S(2)}) %collective-permute-start) | collective-permute-done | bytes 786464 | tf_op jit(solution)/shard_map/while/body/eval_jaxpr/ppermute | solution.py:12
  289.5 13.5 %collective-permute-done = f32[12,128,128]{2,1,0:T(8,128)S(1)} collective-permute-done((f32[12,128,128]{2,1,0:T(8,128)S(1)}, f32[12,128,128]{2,1,0:T(8,128)S(1)}, u32[]{:S(2)}, u32[]{:S(2)}) %collective-permute-start) | collective-permute-done | bytes 786464 | tf_op jit(solution)/shard_map/while/body/eval_jaxpr/ppermute | solution.py:12
  305.0 13.5 %collective-permute-done = f32[12,128,128]{2,1,0:T(8,128)S(1)} collective-permute-done((f32[12,128,128]{2,1,0:T(8,128)S(1)}, f32[12,128,128]{2,1,0:T(8,128)S(1)}, u32[]{:S(2)}, u32[]{:S(2)}) %collective-permute-start) | collective-permute-done | bytes 786464 | tf_op jit(solution)/shard_map/while/body/eval_jaxpr/ppermute | solution.py:12
  320.6 13.5 %collective-permute-done = f32[12,128,128]{2,1,0:T(8,128)S(1)} collective-permute-done((f32[12,128,128]{2,1,0:T(8,128)S(1)}, f32[12,128,128]{2,1,0:T(8,128)S(1)}, u32[]{:S(2)}, u32[]{:S(2)}) %collective-permute-start) | collective-permute-done | bytes 786464 | tf_op jit(solution)/shard_map/while/body/eval_jaxpr/ppermute | solution.py:12
  336.1 13.5 %collective-permute-done = f32[12,128,128]{2,1,0:T(8,128)S(1)} collective-permute-done((f32[12,128,128]{2,1,0:T(8,128)S(1)}, f32[12,128,128]{2,1,0:T(8,128)S(1)}, u32[]{:S(2)}, u32[]{:S(2)}) %collective-permute-start) | collective-permute-done | bytes 786464 | tf_op jit(solution)/shard_map/while/body/eval_jaxpr/ppermute | solution.py:12
  351.7 13.5 %collective-permute-done = f32[12,128,128]{2,1,0:T(8,128)S(1)} collective-permute-done((f32[12,128,128]{2,1,0:T(8,128)S(1)}, f32[12,128,128]{2,1,0:T(8,128)S(1)}, u32[]{:S(2)}, u32[]{:S(2)}) %collective-permute-start) | collective-permute-done | bytes 786464 | tf_op jit(solution)/shard_map/while/body/eval_jaxpr/ppermute | solution.py:12
  367.3 13.5 %collective-permute-done = f32[12,128,128]{2,1,0:T(8,128)S(1)} collective-permute-done((f32[12,128,128]{2,1,0:T(8,128)S(1)}, f32[12,128,128]{2,1,0:T(8,128)S(1)}, u32[]{:S(2)}, u32[]{:S(2)}) %collective-permute-start) | collective-permute-done | bytes 786464 | tf_op jit(solution)/shard_map/while/body/eval_jaxpr/ppermute | solution.py:12
  382.8 13.5 %collective-permute-done = f32[12,128,128]{2,1,0:T(8,128)S(1)} collective-permute-done((f32[12,128,128]{2,1,0:T(8,128)S(1)}, f32[12,128,128]{2,1,0:T(8,128)S(1)}, u32[]{:S(2)}, u32[]{:S(2)}) %collective-permute-start) | collective-permute-done | bytes 786464 | tf_op jit(solution)/shard_map/while/body/eval_jaxpr/ppermute | solution.py:12
  398.4 13.5 %collective-permute-done = f32[12,128,128]{2,1,0:T(8,128)S(1)} collective-permute-done((f32[12,128,128]{2,1,0:T(8,128)S(1)}, f32[12,128,128]{2,1,0:T(8,128)S(1)}, u32[]{:S(2)}, u32[]{:S(2)}) %collective-permute-start) | collective-permute-done | bytes 786464 | tf_op jit(solution)/shard_map/while/body/eval_jaxpr/ppermute | solution.py:12
  414.0 13.5 %collective-permute-done = f32[12,128,128]{2,1,0:T(8,128)S(1)} collective-permute-done((f32[12,128,128]{2,1,0:T(8,128)S(1)}, f32[12,128,128]{2,1,0:T(8,128)S(1)}, u32[]{:S(2)}, u32[]{:S(2)}) %collective-permute-start) | collective-permute-done | bytes 786464 | tf_op jit(solution)/shard_map/while/body/eval_jaxpr/ppermute | solution.py:12
  429.5 13.5 %collective-permute-done = f32[12,128,128]{2,1,0:T(8,128)S(1)} collective-permute-done((f32[12,128,128]{2,1,0:T(8,128)S(1)}, f32[12,128,128]{2,1,0:T(8,128)S(1)}, u32[]{:S(2)}, u32[]{:S(2)}) %collective-permute-start) | collective-permute-done | bytes 786464 | tf_op jit(solution)/shard_map/while/body/eval_jaxpr/ppermute | solution.py:12
  445.1 13.5 %collective-permute-done = f32[12,128,128]{2,1,0:T(8,128)S(1)} collective-permute-done((f32[12,128,128]{2,1,0:T(8,128)S(1)}, f32[12,128,128]{2,1,0:T(8,128)S(1)}, u32[]{:S(2)}, u32[]{:S(2)}) %collective-permute-start) | collective-permute-done | bytes 786464 | tf_op jit(solution)/shard_map/while/body/eval_jaxpr/ppermute | solution.py:12
  460.7 13.5 %collective-permute-done = f32[12,128,128]{2,1,0:T(8,128)S(1)} collective-permute-done((f32[12,128,128]{2,1,0:T(8,128)S(1)}, f32[12,128,128]{2,1,0:T(8,128)S(1)}, u32[]{:S(2)}, u32[]{:S(2)}) %collective-permute-start) | collective-permute-done | bytes 786464 | tf_op jit(solution)/shard_map/while/body/eval_jaxpr/ppermute | solution.py:12
  476.2 13.5 %collective-permute-done = f32[12,128,128]{2,1,0:T(8,128)S(1)} collective-permute-done((f32[12,128,128]{2,1,0:T(8,128)S(1)}, f32[12,128,128]{2,1,0:T(8,128)S(1)}, u32[]{:S(2)}, u32[]{:S(2)}) %collective-permute-start) | collective-permute-done | bytes 786464 | tf_op jit(solution)/shard_map/while/body/eval_jaxpr/ppermute | solution.py:12
  491.8 13.5 %collective-permute-done = f32[12,128,128]{2,1,0:T(8,128)S(1)} collective-permute-done((f32[12,128,128]{2,1,0:T(8,128)S(1)}, f32[12,128,128]{2,1,0:T(8,128)S(1)}, u32[]{:S(2)}, u32[]{:S(2)}) %collective-permute-start) | collective-permute-done | bytes 786464 | tf_op jit(solution)/shard_map/while/body/eval_jaxpr/ppermute | solution.py:12
  507.4 13.5 %collective-permute-done = f32[12,128,128]{2,1,0:T(8,128)S(1)} collective-permute-done((f32[12,128,128]{2,1,0:T(8,128)S(1)}, f32[12,128,128]{2,1,0:T(8,128)S(1)}, u32[]{:S(2)}, u32[]{:S(2)}) %collective-permute-start) | collective-permute-done | bytes 786464 | tf_op jit(solution)/shard_map/while/body/eval_jaxpr/ppermute | solution.py:12
  522.9 13.5 %collective-permute-done = f32[12,128,128]{2,1,0:T(8,128)S(1)} collective-permute-done((f32[12,128,128]{2,1,0:T(8,128)S(1)}, f32[12,128,128]{2,1,0:T(8,128)S(1)}, u32[]{:S(2)}, u32[]{:S(2)}) %collective-permute-start) | collective-permute-done | bytes 786464 | tf_op jit(solution)/shard_map/while/body/eval_jaxpr/ppermute | solution.py:12
  536.4 2.5 fusion.32
  538.9 5.1 multiply_reduce_fusion
  545.5 4.4 fusion.9
  549.9 6.0 %fusion.46 = (bf16[8,256,768]{2,1,0:T(8,128)(2,1)}, bf16[8,256,768]{2,1,0:T(8,128)(2,1)}) fusion(bf16[8,256,1536]{2,1,0:T(8,128)(2,1)} %all-gather.2.cloned.1.call-done), kind=kLoop, calls=%fused_computation.78 | loop fusion | bytes 12582912 | tf_op jit(solution)/shard_map/slice | solution.py:99
  555.9 3.2 copy.37
  559.1 4.7 copy.35
  563.7 2.8 fusion.14
  568.4 4.2 fusion.13
  (138 shorter events, 82.5 us)
Async XLA Ops:
  6.5 27.3 %copy-start = (bf16[1536,12]{0,1:T(8,128)(2,1)S(1)}, bf16[1536,12]{0,1:T(8,128)(2,1)}, u32[]{:S(2)}) copy-start(bf16[1536,12]{0,1:T(8,128)(2,1)} %param.11) | copy-start | bytes 110596
  6.5 543.4 %all-gather.2.cloned.1.call-start = ((), (), s32[]{:S(2)}) async-start(), calls=%async_computation | async-start | bytes 7864320 | tf_op jit(solution)/shard_map/all_gather | solution.py:97
  28.5 5.0 copy-start.2
  29.4 21.9 %collective-permute-start.1 = (bf16[64,1536]{0,1:T(8,128)(2,1)}, bf16[64,1536]{0,1:T(8,128)(2,1)}, u32[]{:S(2)}, u32[]{:S(2)}) collective-permute-start(bf16[64,1536]{0,1:T(8,128)(2,1)} %pad_maximum_fusion.2), channel_id=1, source_target_pairs={{0,4},{4,8},{8,12},{12,16},{16,20},{20,24},{24,28},{28,32},{32,36}... | collective-permute-start | bytes 589832 | tf_op jit(solution)/shard_map/ppermute | solution.py:12
  32.2 1.6 copy-start.12
  32.2 1.6 copy-start.11
  42.9 1.7 copy-start.4
  44.6 1.6 copy-start.5
  47.8 4.7 copy-start.6
  54.0 15.4 %collective-permute-start = (f32[12,128,128]{2,1,0:T(8,128)S(1)}, f32[12,128,128]{2,1,0:T(8,128)S(1)}, u32[]{:S(2)}, u32[]{:S(2)}) collective-permute-start(f32[12,128,128]{2,1,0:T(8,128)S(1)} %multiply_add_fusion.2), channel_id=1, source_target_pairs={{0,4},{4,8},{8,12},{12,16},{16,20},{20,24},{24,28},{28,32},{32,36}... | collective-permute-start | bytes 2359304 | tf_op jit(solution)/shard_map/while/body/eval_jaxpr/ppermute | solution.py:12
  69.6 15.4 %collective-permute-start = (f32[12,128,128]{2,1,0:T(8,128)S(1)}, f32[12,128,128]{2,1,0:T(8,128)S(1)}, u32[]{:S(2)}, u32[]{:S(2)}) collective-permute-start(f32[12,128,128]{2,1,0:T(8,128)S(1)} %multiply_add_fusion.2), channel_id=1, source_target_pairs={{0,4},{4,8},{8,12},{12,16},{16,20},{20,24},{24,28},{28,32},{32,36}... | collective-permute-start | bytes 2359304 | tf_op jit(solution)/shard_map/while/body/eval_jaxpr/ppermute | solution.py:12
  85.2 15.4 %collective-permute-start = (f32[12,128,128]{2,1,0:T(8,128)S(1)}, f32[12,128,128]{2,1,0:T(8,128)S(1)}, u32[]{:S(2)}, u32[]{:S(2)}) collective-permute-start(f32[12,128,128]{2,1,0:T(8,128)S(1)} %multiply_add_fusion.2), channel_id=1, source_target_pairs={{0,4},{4,8},{8,12},{12,16},{16,20},{20,24},{24,28},{28,32},{32,36}... | collective-permute-start | bytes 2359304 | tf_op jit(solution)/shard_map/while/body/eval_jaxpr/ppermute | solution.py:12
  100.7 15.4 %collective-permute-start = (f32[12,128,128]{2,1,0:T(8,128)S(1)}, f32[12,128,128]{2,1,0:T(8,128)S(1)}, u32[]{:S(2)}, u32[]{:S(2)}) collective-permute-start(f32[12,128,128]{2,1,0:T(8,128)S(1)} %multiply_add_fusion.2), channel_id=1, source_target_pairs={{0,4},{4,8},{8,12},{12,16},{16,20},{20,24},{24,28},{28,32},{32,36}... | collective-permute-start | bytes 2359304 | tf_op jit(solution)/shard_map/while/body/eval_jaxpr/ppermute | solution.py:12
  116.3 15.4 %collective-permute-start = (f32[12,128,128]{2,1,0:T(8,128)S(1)}, f32[12,128,128]{2,1,0:T(8,128)S(1)}, u32[]{:S(2)}, u32[]{:S(2)}) collective-permute-start(f32[12,128,128]{2,1,0:T(8,128)S(1)} %multiply_add_fusion.2), channel_id=1, source_target_pairs={{0,4},{4,8},{8,12},{12,16},{16,20},{20,24},{24,28},{28,32},{32,36}... | collective-permute-start | bytes 2359304 | tf_op jit(solution)/shard_map/while/body/eval_jaxpr/ppermute | solution.py:12
  131.9 15.4 %collective-permute-start = (f32[12,128,128]{2,1,0:T(8,128)S(1)}, f32[12,128,128]{2,1,0:T(8,128)S(1)}, u32[]{:S(2)}, u32[]{:S(2)}) collective-permute-start(f32[12,128,128]{2,1,0:T(8,128)S(1)} %multiply_add_fusion.2), channel_id=1, source_target_pairs={{0,4},{4,8},{8,12},{12,16},{16,20},{20,24},{24,28},{28,32},{32,36}... | collective-permute-start | bytes 2359304 | tf_op jit(solution)/shard_map/while/body/eval_jaxpr/ppermute | solution.py:12
  147.4 15.4 %collective-permute-start = (f32[12,128,128]{2,1,0:T(8,128)S(1)}, f32[12,128,128]{2,1,0:T(8,128)S(1)}, u32[]{:S(2)}, u32[]{:S(2)}) collective-permute-start(f32[12,128,128]{2,1,0:T(8,128)S(1)} %multiply_add_fusion.2), channel_id=1, source_target_pairs={{0,4},{4,8},{8,12},{12,16},{16,20},{20,24},{24,28},{28,32},{32,36}... | collective-permute-start | bytes 2359304 | tf_op jit(solution)/shard_map/while/body/eval_jaxpr/ppermute | solution.py:12
  163.0 15.4 %collective-permute-start = (f32[12,128,128]{2,1,0:T(8,128)S(1)}, f32[12,128,128]{2,1,0:T(8,128)S(1)}, u32[]{:S(2)}, u32[]{:S(2)}) collective-permute-start(f32[12,128,128]{2,1,0:T(8,128)S(1)} %multiply_add_fusion.2), channel_id=1, source_target_pairs={{0,4},{4,8},{8,12},{12,16},{16,20},{20,24},{24,28},{28,32},{32,36}... | collective-permute-start | bytes 2359304 | tf_op jit(solution)/shard_map/while/body/eval_jaxpr/ppermute | solution.py:12
  178.6 15.4 %collective-permute-start = (f32[12,128,128]{2,1,0:T(8,128)S(1)}, f32[12,128,128]{2,1,0:T(8,128)S(1)}, u32[]{:S(2)}, u32[]{:S(2)}) collective-permute-start(f32[12,128,128]{2,1,0:T(8,128)S(1)} %multiply_add_fusion.2), channel_id=1, source_target_pairs={{0,4},{4,8},{8,12},{12,16},{16,20},{20,24},{24,28},{28,32},{32,36}... | collective-permute-start | bytes 2359304 | tf_op jit(solution)/shard_map/while/body/eval_jaxpr/ppermute | solution.py:12
  194.1 15.4 %collective-permute-start = (f32[12,128,128]{2,1,0:T(8,128)S(1)}, f32[12,128,128]{2,1,0:T(8,128)S(1)}, u32[]{:S(2)}, u32[]{:S(2)}) collective-permute-start(f32[12,128,128]{2,1,0:T(8,128)S(1)} %multiply_add_fusion.2), channel_id=1, source_target_pairs={{0,4},{4,8},{8,12},{12,16},{16,20},{20,24},{24,28},{28,32},{32,36}... | collective-permute-start | bytes 2359304 | tf_op jit(solution)/shard_map/while/body/eval_jaxpr/ppermute | solution.py:12
  209.7 15.4 %collective-permute-start = (f32[12,128,128]{2,1,0:T(8,128)S(1)}, f32[12,128,128]{2,1,0:T(8,128)S(1)}, u32[]{:S(2)}, u32[]{:S(2)}) collective-permute-start(f32[12,128,128]{2,1,0:T(8,128)S(1)} %multiply_add_fusion.2), channel_id=1, source_target_pairs={{0,4},{4,8},{8,12},{12,16},{16,20},{20,24},{24,28},{28,32},{32,36}... | collective-permute-start | bytes 2359304 | tf_op jit(solution)/shard_map/while/body/eval_jaxpr/ppermute | solution.py:12
  225.3 15.4 %collective-permute-start = (f32[12,128,128]{2,1,0:T(8,128)S(1)}, f32[12,128,128]{2,1,0:T(8,128)S(1)}, u32[]{:S(2)}, u32[]{:S(2)}) collective-permute-start(f32[12,128,128]{2,1,0:T(8,128)S(1)} %multiply_add_fusion.2), channel_id=1, source_target_pairs={{0,4},{4,8},{8,12},{12,16},{16,20},{20,24},{24,28},{28,32},{32,36}... | collective-permute-start | bytes 2359304 | tf_op jit(solution)/shard_map/while/body/eval_jaxpr/ppermute | solution.py:12
  240.8 15.4 %collective-permute-start = (f32[12,128,128]{2,1,0:T(8,128)S(1)}, f32[12,128,128]{2,1,0:T(8,128)S(1)}, u32[]{:S(2)}, u32[]{:S(2)}) collective-permute-start(f32[12,128,128]{2,1,0:T(8,128)S(1)} %multiply_add_fusion.2), channel_id=1, source_target_pairs={{0,4},{4,8},{8,12},{12,16},{16,20},{20,24},{24,28},{28,32},{32,36}... | collective-permute-start | bytes 2359304 | tf_op jit(solution)/shard_map/while/body/eval_jaxpr/ppermute | solution.py:12
  256.4 15.4 %collective-permute-start = (f32[12,128,128]{2,1,0:T(8,128)S(1)}, f32[12,128,128]{2,1,0:T(8,128)S(1)}, u32[]{:S(2)}, u32[]{:S(2)}) collective-permute-start(f32[12,128,128]{2,1,0:T(8,128)S(1)} %multiply_add_fusion.2), channel_id=1, source_target_pairs={{0,4},{4,8},{8,12},{12,16},{16,20},{20,24},{24,28},{28,32},{32,36}... | collective-permute-start | bytes 2359304 | tf_op jit(solution)/shard_map/while/body/eval_jaxpr/ppermute | solution.py:12
  272.0 15.4 %collective-permute-start = (f32[12,128,128]{2,1,0:T(8,128)S(1)}, f32[12,128,128]{2,1,0:T(8,128)S(1)}, u32[]{:S(2)}, u32[]{:S(2)}) collective-permute-start(f32[12,128,128]{2,1,0:T(8,128)S(1)} %multiply_add_fusion.2), channel_id=1, source_target_pairs={{0,4},{4,8},{8,12},{12,16},{16,20},{20,24},{24,28},{28,32},{32,36}... | collective-permute-start | bytes 2359304 | tf_op jit(solution)/shard_map/while/body/eval_jaxpr/ppermute | solution.py:12
  287.5 15.4 %collective-permute-start = (f32[12,128,128]{2,1,0:T(8,128)S(1)}, f32[12,128,128]{2,1,0:T(8,128)S(1)}, u32[]{:S(2)}, u32[]{:S(2)}) collective-permute-start(f32[12,128,128]{2,1,0:T(8,128)S(1)} %multiply_add_fusion.2), channel_id=1, source_target_pairs={{0,4},{4,8},{8,12},{12,16},{16,20},{20,24},{24,28},{28,32},{32,36}... | collective-permute-start | bytes 2359304 | tf_op jit(solution)/shard_map/while/body/eval_jaxpr/ppermute | solution.py:12
  303.1 15.4 %collective-permute-start = (f32[12,128,128]{2,1,0:T(8,128)S(1)}, f32[12,128,128]{2,1,0:T(8,128)S(1)}, u32[]{:S(2)}, u32[]{:S(2)}) collective-permute-start(f32[12,128,128]{2,1,0:T(8,128)S(1)} %multiply_add_fusion.2), channel_id=1, source_target_pairs={{0,4},{4,8},{8,12},{12,16},{16,20},{20,24},{24,28},{28,32},{32,36}... | collective-permute-start | bytes 2359304 | tf_op jit(solution)/shard_map/while/body/eval_jaxpr/ppermute | solution.py:12
  318.6 15.4 %collective-permute-start = (f32[12,128,128]{2,1,0:T(8,128)S(1)}, f32[12,128,128]{2,1,0:T(8,128)S(1)}, u32[]{:S(2)}, u32[]{:S(2)}) collective-permute-start(f32[12,128,128]{2,1,0:T(8,128)S(1)} %multiply_add_fusion.2), channel_id=1, source_target_pairs={{0,4},{4,8},{8,12},{12,16},{16,20},{20,24},{24,28},{28,32},{32,36}... | collective-permute-start | bytes 2359304 | tf_op jit(solution)/shard_map/while/body/eval_jaxpr/ppermute | solution.py:12
  334.2 15.4 %collective-permute-start = (f32[12,128,128]{2,1,0:T(8,128)S(1)}, f32[12,128,128]{2,1,0:T(8,128)S(1)}, u32[]{:S(2)}, u32[]{:S(2)}) collective-permute-start(f32[12,128,128]{2,1,0:T(8,128)S(1)} %multiply_add_fusion.2), channel_id=1, source_target_pairs={{0,4},{4,8},{8,12},{12,16},{16,20},{20,24},{24,28},{28,32},{32,36}... | collective-permute-start | bytes 2359304 | tf_op jit(solution)/shard_map/while/body/eval_jaxpr/ppermute | solution.py:12
  349.8 15.4 %collective-permute-start = (f32[12,128,128]{2,1,0:T(8,128)S(1)}, f32[12,128,128]{2,1,0:T(8,128)S(1)}, u32[]{:S(2)}, u32[]{:S(2)}) collective-permute-start(f32[12,128,128]{2,1,0:T(8,128)S(1)} %multiply_add_fusion.2), channel_id=1, source_target_pairs={{0,4},{4,8},{8,12},{12,16},{16,20},{20,24},{24,28},{28,32},{32,36}... | collective-permute-start | bytes 2359304 | tf_op jit(solution)/shard_map/while/body/eval_jaxpr/ppermute | solution.py:12
  365.3 15.4 %collective-permute-start = (f32[12,128,128]{2,1,0:T(8,128)S(1)}, f32[12,128,128]{2,1,0:T(8,128)S(1)}, u32[]{:S(2)}, u32[]{:S(2)}) collective-permute-start(f32[12,128,128]{2,1,0:T(8,128)S(1)} %multiply_add_fusion.2), channel_id=1, source_target_pairs={{0,4},{4,8},{8,12},{12,16},{16,20},{20,24},{24,28},{28,32},{32,36}... | collective-permute-start | bytes 2359304 | tf_op jit(solution)/shard_map/while/body/eval_jaxpr/ppermute | solution.py:12
  380.9 15.4 %collective-permute-start = (f32[12,128,128]{2,1,0:T(8,128)S(1)}, f32[12,128,128]{2,1,0:T(8,128)S(1)}, u32[]{:S(2)}, u32[]{:S(2)}) collective-permute-start(f32[12,128,128]{2,1,0:T(8,128)S(1)} %multiply_add_fusion.2), channel_id=1, source_target_pairs={{0,4},{4,8},{8,12},{12,16},{16,20},{20,24},{24,28},{28,32},{32,36}... | collective-permute-start | bytes 2359304 | tf_op jit(solution)/shard_map/while/body/eval_jaxpr/ppermute | solution.py:12
  396.5 15.4 %collective-permute-start = (f32[12,128,128]{2,1,0:T(8,128)S(1)}, f32[12,128,128]{2,1,0:T(8,128)S(1)}, u32[]{:S(2)}, u32[]{:S(2)}) collective-permute-start(f32[12,128,128]{2,1,0:T(8,128)S(1)} %multiply_add_fusion.2), channel_id=1, source_target_pairs={{0,4},{4,8},{8,12},{12,16},{16,20},{20,24},{24,28},{28,32},{32,36}... | collective-permute-start | bytes 2359304 | tf_op jit(solution)/shard_map/while/body/eval_jaxpr/ppermute | solution.py:12
  412.0 15.4 %collective-permute-start = (f32[12,128,128]{2,1,0:T(8,128)S(1)}, f32[12,128,128]{2,1,0:T(8,128)S(1)}, u32[]{:S(2)}, u32[]{:S(2)}) collective-permute-start(f32[12,128,128]{2,1,0:T(8,128)S(1)} %multiply_add_fusion.2), channel_id=1, source_target_pairs={{0,4},{4,8},{8,12},{12,16},{16,20},{20,24},{24,28},{28,32},{32,36}... | collective-permute-start | bytes 2359304 | tf_op jit(solution)/shard_map/while/body/eval_jaxpr/ppermute | solution.py:12
  427.6 15.4 %collective-permute-start = (f32[12,128,128]{2,1,0:T(8,128)S(1)}, f32[12,128,128]{2,1,0:T(8,128)S(1)}, u32[]{:S(2)}, u32[]{:S(2)}) collective-permute-start(f32[12,128,128]{2,1,0:T(8,128)S(1)} %multiply_add_fusion.2), channel_id=1, source_target_pairs={{0,4},{4,8},{8,12},{12,16},{16,20},{20,24},{24,28},{28,32},{32,36}... | collective-permute-start | bytes 2359304 | tf_op jit(solution)/shard_map/while/body/eval_jaxpr/ppermute | solution.py:12
  443.2 15.4 %collective-permute-start = (f32[12,128,128]{2,1,0:T(8,128)S(1)}, f32[12,128,128]{2,1,0:T(8,128)S(1)}, u32[]{:S(2)}, u32[]{:S(2)}) collective-permute-start(f32[12,128,128]{2,1,0:T(8,128)S(1)} %multiply_add_fusion.2), channel_id=1, source_target_pairs={{0,4},{4,8},{8,12},{12,16},{16,20},{20,24},{24,28},{28,32},{32,36}... | collective-permute-start | bytes 2359304 | tf_op jit(solution)/shard_map/while/body/eval_jaxpr/ppermute | solution.py:12
  458.7 15.4 %collective-permute-start = (f32[12,128,128]{2,1,0:T(8,128)S(1)}, f32[12,128,128]{2,1,0:T(8,128)S(1)}, u32[]{:S(2)}, u32[]{:S(2)}) collective-permute-start(f32[12,128,128]{2,1,0:T(8,128)S(1)} %multiply_add_fusion.2), channel_id=1, source_target_pairs={{0,4},{4,8},{8,12},{12,16},{16,20},{20,24},{24,28},{28,32},{32,36}... | collective-permute-start | bytes 2359304 | tf_op jit(solution)/shard_map/while/body/eval_jaxpr/ppermute | solution.py:12
  474.3 15.4 %collective-permute-start = (f32[12,128,128]{2,1,0:T(8,128)S(1)}, f32[12,128,128]{2,1,0:T(8,128)S(1)}, u32[]{:S(2)}, u32[]{:S(2)}) collective-permute-start(f32[12,128,128]{2,1,0:T(8,128)S(1)} %multiply_add_fusion.2), channel_id=1, source_target_pairs={{0,4},{4,8},{8,12},{12,16},{16,20},{20,24},{24,28},{28,32},{32,36}... | collective-permute-start | bytes 2359304 | tf_op jit(solution)/shard_map/while/body/eval_jaxpr/ppermute | solution.py:12
  489.9 15.4 %collective-permute-start = (f32[12,128,128]{2,1,0:T(8,128)S(1)}, f32[12,128,128]{2,1,0:T(8,128)S(1)}, u32[]{:S(2)}, u32[]{:S(2)}) collective-permute-start(f32[12,128,128]{2,1,0:T(8,128)S(1)} %multiply_add_fusion.2), channel_id=1, source_target_pairs={{0,4},{4,8},{8,12},{12,16},{16,20},{20,24},{24,28},{28,32},{32,36}... | collective-permute-start | bytes 2359304 | tf_op jit(solution)/shard_map/while/body/eval_jaxpr/ppermute | solution.py:12
  505.4 15.4 %collective-permute-start = (f32[12,128,128]{2,1,0:T(8,128)S(1)}, f32[12,128,128]{2,1,0:T(8,128)S(1)}, u32[]{:S(2)}, u32[]{:S(2)}) collective-permute-start(f32[12,128,128]{2,1,0:T(8,128)S(1)} %multiply_add_fusion.2), channel_id=1, source_target_pairs={{0,4},{4,8},{8,12},{12,16},{16,20},{20,24},{24,28},{28,32},{32,36}... | collective-permute-start | bytes 2359304 | tf_op jit(solution)/shard_map/while/body/eval_jaxpr/ppermute | solution.py:12
  521.0 15.4 %collective-permute-start = (f32[12,128,128]{2,1,0:T(8,128)S(1)}, f32[12,128,128]{2,1,0:T(8,128)S(1)}, u32[]{:S(2)}, u32[]{:S(2)}) collective-permute-start(f32[12,128,128]{2,1,0:T(8,128)S(1)} %multiply_add_fusion.2), channel_id=1, source_target_pairs={{0,4},{4,8},{8,12},{12,16},{16,20},{20,24},{24,28},{28,32},{32,36}... | collective-permute-start | bytes 2359304 | tf_op jit(solution)/shard_map/while/body/eval_jaxpr/ppermute | solution.py:12
  536.4 2.5 copy-start.9
  536.4 2.5 copy-start.10
  538.9 5.7 slice-start
  538.9 5.7 slice-start.1
  544.1 1.4 copy-start.3
  563.7 2.8 copy-start.7
  566.5 1.9 copy-start.13
  568.1 4.5 copy-start.1
  (1 other events, 1.2 us)
Sparse Core Ops, SparseCore 0:
  53.9 68.6 all-gather.1
where the time goes:
time: 581 us; the launch traced here: 579 us
  waiting for transfers between devices  417 us (72%)
  starting transfers between devices  63 us (11%)
  matrix products  35.6 us (6%)
  local copies, waits for them, and re-layouts  33.7 us (6%)
  other arithmetic  16.2 us (3%)
  between operations  13.7 us (2%)
    ppermute x32, waiting for transfers between devices, shifted(): lax.ppermute(value, axis, [(source, source + steps) for source in range(l...  416 us
    ppermute x32, starting transfers between devices, shifted(): lax.ppermute(value, axis, [(source, source + steps) for source in range(l...  63 us
    unnamed x35, local copies, waits for them, and re-layouts  12.7 us
  transfers between devices with their start and end apart: 33, of which 31 were waited for; matrix products, arithmetic and copies ran while one was open for 6% of the time, Pallas kernels for 0%

commit v1 on v0

v1 whole, which is shorter than its diff:
```python
import math

import jax
import jax.numpy as jnp
from jax import lax
from jax.experimental import pallas as pl
from jax.experimental.pallas import tpu as pltpu
from jax.sharding import PartitionSpec as P

MESH = pl.DeviceIdType.MESH
BF = jnp.bfloat16
F32 = jnp.float32
EXACT = lax.Precision.HIGHEST

D = 1536
H = 12
HP = 128
N = 128
AH = 6
AW = AH * HP
FR = 8
BLK = 64
ROWS = FR * BLK
POS = 256
CH = 128
NCH = ROWS // CH
TM = 32
TILE = 256


def per_head(cols):
    rows = cols.shape[0]
    return jnp.concatenate(
        [jnp.broadcast_to(cols[:, h : h + 1], (rows, HP)) for h in range(H)], axis=1
    )


def twice(v):
    return jnp.concatenate([v, v], axis=1)


def inv_rms(x, eps):
    x = x.astype(F32)
    mean = jnp.sum(x * x, axis=-1, keepdims=True) * (1.0 / x.shape[-1])
    return jnp.broadcast_to(lax.rsqrt(mean + eps), (x.shape[0], 128))


def head_scaled(v, eps):
    halves = [v[:, :HP], v[:, HP:]]
    return jnp.concatenate([p * inv_rms(p, eps) for p in halves], axis=1)


def kernel(
    lat, wm_h, ws_h, bias_ref, rate_ref, wa_h, wo_h, out_h,
    xv, xt, wm, ws, wa, wo, u, yv, acc, ob, ssm,
    kv, qt, qe, at_send, at_recv,
    r_ref, rt_ref, la_ref, lat_t, dt_t,
    s_ref, s_k, l_bf, a_recv, t_bf, b_recv, i_ref, p_bf, c_recv, d_send, d_recv, e_send, s_in,
    ld_own, ld_a, ld_t, ld_b, ld_p, ld_c,
    load_sem, own_sem, x_ssem, x_rsem, q_ssem, q_rsem, at_ssem, at_rsem,
    a_ssem, a_rsem, b_ssem, b_rsem, c_ssem, c_rsem, d_ssem, d_rsem, e_ssem, e_rsem,
):
    t = lax.axis_index("tm")
    y = lax.axis_index("space")
    core = lax.rem(t, 2)
    x = lax.rem(lax.div(t, 2), 4)
    z = lax.div(t, 8)
    t_next = lax.rem(t + 1, TM)
    t_prev = lax.rem(t + TM - 1, TM)
    ys = [lax.rem(y + d, 4) for d in range(4)]
    mate = (t + 1 - 2 * core, y)
    xs = [lax.rem(x + d, 4) for d in range(4)]
    x_dev = [(z * 8 + xs[d] * 2 + core, y) for d in range(4)]
    z_dev = [(lax.rem(z + d, 4) * 8 + x * 2 + core, y) for d in range(4)]
    last = y == 3

    def remote(src, dst, ssem, rsem, dev):
        return pltpu.make_async_remote_copy(
            src_ref=src, dst_ref=dst, send_sem=ssem, recv_sem=rsem,
            device_id=dev, device_id_type=MESH,
        )

    loads = [
        pltpu.make_async_copy(src, dst, load_sem.at[i])
        for i, (src, dst) in enumerate([(lat, xv), (ws_h, ws), (wm_h, wm), (wa_h, wa), (wo_h, wo)])
    ]
    for i in (0, 1, 2):
        loads[i].start()

    barrier = pltpu.get_barrier_semaphore()

    def greet(dev):
        pl.semaphore_signal(barrier, inc=1, device_id=dev, device_id_type=MESH)

    for d in (1, 2, 3):
        greet((t, ys[d]))
        greet(x_dev[d])
        greet(z_dev[d])
    greet(mate)
    greet((t_prev, 3))

    @pl.when(last)
    def _():
        for k in range(4):
            greet((t_next, k))

    pl.semaphore_wait(barrier, 11 + 4 * jnp.where(last, 1, 0))

    def x_copy(i, d):
        return remote(
            lat.at[pl.ds(pl.multiple_of(128 * ys[d] + 64 * i, 64), 64), :],
            xt.at[i, pl.ds(pl.multiple_of(64 * y, 64), 64), :],
            x_ssem.at[i, d], x_rsem.at[i, d], (t, ys[d]),
        )

    def x_own(i):
        return pltpu.make_async_copy(
            lat.at[pl.ds(pl.multiple_of(128 * y + 64 * i, 64), 64), :],
            xt.at[i, pl.ds(pl.multiple_of(64 * y, 64), 64), :],
            own_sem.at[i],
        )

    for i in range(2):
        for d in (2, 1, 3):
            x_copy(i, d).start()
        x_own(i).start()
    loads[3].start()
    loads[4].start()

    loads[0].wait()

    def norm_rows(j, _):
        rs = pl.ds(pl.multiple_of(j * 64, 64), 64)
        r_ref[rs, :] = inv_rms(xv[rs, :], 1e-6)
        return 0

    lax.fori_loop(0, ROWS // 64, norm_rows, 0)
    loads[1].wait()
    loads[2].wait()

    steps = jnp.dot(xv[...], ws[...], preferred_element_type=F32)
    steps = steps * r_ref[:, :H] + bias_ref[...]
    dt = jnp.maximum(steps, 0.0) + jnp.log(1.0 + jnp.exp(-jnp.abs(steps)))
    rate = rate_ref[...]
    row_id = lax.broadcasted_iota(jnp.int32, (CH, CH), 0)
    col_id = lax.broadcasted_iota(jnp.int32, (CH, CH), 1)
    causal = row_id >= col_id
    tri = jnp.where(causal, 1.0, 0.0).astype(F32)
    eye = jnp.where(row_id == col_id, 1.0, 0.0).astype(F32)
    offs = [jnp.zeros((1, H), F32)]
    ends = []
    fe = []
    for k in range(NCH):
        dt_k = dt[k * CH : (k + 1) * CH, :]
        a_k = -rate * dt_k
        la_k = jnp.dot(tri, a_k, precision=EXACT, preferred_element_type=F32)
        la_ref[k * CH : (k + 1) * CH, :] = la_k
        lat_t[k] = lax.dot_general(
            a_k, tri, (((0,), (1,)), ((), ())), precision=EXACT, preferred_element_type=F32
        )
        dt_t[k] = lax.dot_general(
            dt_k, eye, (((0,), (1,)), ((), ())), precision=EXACT, preferred_element_type=F32
        )
        end_k = la_k[CH - 1 : CH, :]
        ends.append(end_k)
        offs.append(offs[-1] + end_k)
        fe.append(jnp.exp(end_k - la_k) * dt_k)
    ld_own[...] = jnp.zeros((8, 128), F32)
    ld_t[...] = jnp.zeros((8, 128), F32)
    ld_p[...] = jnp.zeros((8, 128), F32)
    ld_own[0:1, 0:H] = offs[NCH]

    def mix(j, _):
        cs = pl.ds(pl.multiple_of(j * TILE, TILE), TILE)
        part = jnp.dot(xv[...], wm[:, cs], preferred_element_type=F32)
        u[:, cs] = (part * twice(r_ref[...])).astype(BF)
        return 0

    lax.fori_loop(0, (D + 2 * N) // TILE, mix, 0)

    loads[3].wait()

    def q_even(j, _):
        cs = pl.ds(pl.multiple_of(j * TILE, TILE), TILE)
        rows = xv[...].reshape(4, 2, BLK, D)[:, 0].reshape(4 * BLK, D)
        scale = r_ref[...].reshape(4, 2, BLK, 128)[:, 0].reshape(4 * BLK, 128)
        part = jnp.dot(rows, wa[:, cs], preferred_element_type=F32) * twice(scale)
        qe[:, :, cs] = head_scaled(part, 1e-6).astype(BF).reshape(4, BLK, TILE)
        return 0

    lax.fori_loop(0, AW // TILE, q_even, 0)

    def q_copy(k):
        dev = (t_prev, 3) if k == 0 else (t, k - 1)
        return remote(
            qe.at[k], qt.at[1, pl.ds(pl.multiple_of(64 * y, 64), 64), :],
            q_ssem.at[k], q_rsem.at[y], dev,
        )

    def q_own(k):
        return pltpu.make_async_copy(
            qe.at[k], qt.at[1, pl.ds(pl.multiple_of(64 * y, 64), 64), :], q_rsem.at[y]
        )

    q_copy(0).start()
    for k in (1, 2, 3):

        @pl.when(y != k - 1)
        def _(k=k):
            q_copy(k).start()

        @pl.when(y == k - 1)
        def _(k=k):
            q_own(k).start()

    for k in range(NCH):
        rs = pl.ds(k * CH, CH)
        scaled = (per_head(fe[k]) * u[rs, :D].astype(F32)).astype(BF)
        add = lax.dot_general(
            u[rs, D : D + N], scaled, (((0,), (0,)), ((), ())), preferred_element_type=F32
        )
        if k == 0:
            s_k[0] = jnp.zeros((N, D), BF)
            s_ref[...] = add
        else:
            s_k[k] = s_ref[...].astype(BF)
            s_ref[...] = s_ref[...] * per_head(jnp.exp(ends[k])) + add
    l_bf[...] = s_ref[...].astype(BF)

    half = pl.ds(pl.multiple_of(64 * core, 64), 64)
    other_half = pl.ds(pl.multiple_of(64 - 64 * core, 64), 64)
    a_copies = [
        remote(l_bf.at[other_half, :], a_recv, a_ssem.at[0], a_rsem.at[0], mate),
        remote(ld_own, ld_a, a_ssem.at[1], a_rsem.at[1], mate),
    ]
    for cp in a_copies:
        cp.start()

    def diag(k, _):
        rs = pl.ds(pl.multiple_of(k * CH, CH), CH)
        cb = lax.dot_general(
            u[rs, D + N : D + 2 * N], u[rs, D : D + N], (((1,), (1,)), ((), ())),
            preferred_element_type=F32,
        )
        la_k = la_ref[rs, :]
        la_row = lat_t[k]
        dt_row = dt_t[k]
        for h in range(H):
            gap = la_k[:, h : h + 1] - la_row[h : h + 1, :]
            w = jnp.exp(jnp.where(causal, gap, -1e30)) * cb * dt_row[h : h + 1, :]
            yv[rs, h * HP : (h + 1) * HP] = jnp.dot(
                w.astype(BF), u[rs, h * HP : (h + 1) * HP], preferred_element_type=F32
            )
        return 0

    lax.fori_loop(0, 2, diag, 0)

    for cp in a_copies:
        cp.wait()
    first = core == 0
    mine = s_ref[half, :]
    theirs = a_recv[...].astype(F32)
    l0 = jnp.where(first, mine, theirs)
    l1 = jnp.where(first, theirs, mine)
    ld_mine = ld_own[0:1, 0:H]
    ld_theirs = ld_a[0:1, 0:H]
    ld0 = jnp.where(first, ld_mine, ld_theirs)
    ld1 = jnp.where(first, ld_theirs, ld_mine)
    t_bf[...] = (per_head(jnp.exp(ld1)) * l0 + l1).astype(BF)
    ld_t[0:1, 0:H] = ld0 + ld1
    b_recv[x] = t_bf[pl.ds(pl.multiple_of(16 * x, 16), 16), :]
    ld_b[x] = ld_t[...]
    b_copies = []
    for d in (1, 2, 3):
        part = t_bf.at[pl.ds(pl.multiple_of(16 * xs[d], 16), 16), :]
        b_copies.append(remote(part, b_recv.at[x], b_ssem.at[0, d], b_rsem.at[0, d], x_dev[d]))
        b_copies.append(remote(ld_t, ld_b.at[x], b_ssem.at[1, d], b_rsem.at[1, d], x_dev[d]))
    for cp in b_copies:
        cp.start()

    lax.fori_loop(2, 4, diag, 0)

    for cp in b_copies:
        cp.wait()
    run = jnp.zeros((16, D), F32)
    ld_sum = jnp.zeros((1, H), F32)
    x_offs = []
    for j in range(4):
        i_ref[j] = run
        x_offs.append(ld_sum)
        ld_j = ld_b[j][0:1, 0:H]
        run = run * per_head(jnp.exp(ld_j)) + b_recv[j].astype(F32)
        ld_sum = ld_sum + ld_j
    p_bf[...] = run.astype(BF)
    ld_p[0:1, 0:H] = ld_sum
    c_recv[z] = p_bf[...]
    ld_c[z] = ld_p[...]
    c_copies = []
    for d in (1, 2, 3):
        c_copies.append(remote(p_bf, c_recv.at[z], c_ssem.at[0, d], c_rsem.at[0, d], z_dev[d]))
        c_copies.append(remote(ld_p, ld_c.at[z], c_ssem.at[1, d], c_rsem.at[1, d], z_dev[d]))
    for cp in c_copies:
        cp.start()

    def attend_proj(i, width_from, dst, dst_from, tiles, scaled_tiles):
        def body(j, _):
            src = pl.ds(pl.multiple_of(width_from + j * TILE, TILE), TILE)
            to = pl.ds(pl.multiple_of(dst_from + j * TILE, TILE), TILE)
            part = jnp.dot(xt[i], wa[:, src], preferred_element_type=F32)
            part = part * twice(rt_ref[...])
            if scaled_tiles:
                part = head_scaled(part, 1e-6)
            dst[i, :, to] = part.astype(BF)
            return 0

        lax.fori_loop(0, tiles, body, 0)

    def norm_frame(i):
        def body(j, _):
            rs = pl.ds(pl.multiple_of(j * 64, 64), 64)
            rt_ref[rs, :] = inv_rms(xt[i, rs, :], 1e-6)
            return 0

        lax.fori_loop(0, POS // 64, body, 0)

    def frame_arrived(i):
        for d in (1, 2, 3):
            x_copy(i, d).wait_recv()
        x_own(i).wait()

    frame_arrived(0)
    norm_frame(0)
    attend_proj(0, AW, kv, 0, 3, True)
    attend_proj(0, 2 * AW, kv, AW, 3, False)

    for cp in c_copies:
        cp.wait()
    run = jnp.zeros((16, D), F32)
    for j in range(4):
        nxt = run * per_head(jnp.exp(ld_c[j][0:1, 0:H])) + c_recv[j].astype(F32)
        run = jnp.where(j < z, nxt, run)
    for j in range(4):
        d_send[j] = (run * per_head(jnp.exp(x_offs[j])) + i_ref[j]).astype(BF)
    d_recv[x] = d_send[x]
    d_copies = [
        remote(d_send.at[xs[d]], d_recv.at[x], d_ssem.at[d], d_rsem.at[d], x_dev[d])
        for d in (1, 2, 3)
    ]
    for cp in d_copies:
        cp.start()

    frame_arrived(1)
    norm_frame(1)

    for cp in d_copies:
        cp.wait()
    inc0 = d_recv[...].astype(F32).reshape(64, D)
    inc1 = per_head(jnp.exp(ld0)) * inc0 + l0
    e_send[...] = jnp.where(first, inc1, inc0).astype(BF)
    s_in[half, :] = jnp.where(first, inc0, inc1).astype(BF)
    e_copy = remote(e_send, s_in.at[half, :], e_ssem, e_rsem, mate)
    e_copy.start()

    def q_odd(j, _):
        cs = pl.ds(pl.multiple_of(j * TILE, TILE), TILE)
        part = jnp.dot(xt[1], wa[:, cs], preferred_element_type=F32) * twice(rt_ref[...])
        qt[0, :, cs] = head_scaled(part, 1e-6).astype(BF)
        return 0

    lax.fori_loop(0, 3, q_odd, 0)

    def attention(i):
        for h in range(AH):
            hs = slice(h * HP, (h + 1) * HP)
            vs = slice(AW + h * HP, AW + (h + 1) * HP)
            s = lax.dot_general(
                qt[i, :, hs], kv[i, :, hs], (((1,), (1,)), ((), ())), preferred_element_type=F32
            )
            p = jnp.exp(s * (1.0 / math.sqrt(HP)))
            total = jnp.sum(p, axis=-1, keepdims=True)
            num = jnp.dot(p.astype(BF), kv[i, :, vs], preferred_element_type=F32)
            at_send[i, :, hs] = (num / total).astype(BF)

    def at_copy(i, d):
        src = at_send.at[i, pl.ds(pl.multiple_of(64 * ys[d], 64), 64), :]
        if i == 0:
            return remote(src, at_recv.at[1, y], at_ssem.at[i, d], at_rsem.at[1, y], (t, ys[d]))
        owner = jnp.where(last, t_next, t)
        k = ys[1]
        return remote(src, at_recv.at[0, k], at_ssem.at[i, d], at_rsem.at[0, k], (owner, ys[d]))

    def at_own(i):
        src = at_send.at[i, pl.ds(pl.multiple_of(64 * y, 64), 64), :]
        if i == 0:
            return pltpu.make_async_copy(src, at_recv.at[1, y], at_rsem.at[1, y])
        return pltpu.make_async_copy(src, at_recv.at[0, ys[1]], at_rsem.at[0, ys[1]])

    attention(0)
    for d in (2, 1, 3):
        at_copy(0, d).start()
    at_own(0).start()

    attend_proj(1, AW, kv, 0, 3, True)
    attend_proj(1, 2 * AW, kv, AW, 3, False)
    for k in range(4):
        pltpu.make_async_copy(qe.at[k], qt.at[1, pl.ds(64 * k, 64), :], q_rsem.at[k]).wait()
    attention(1)
    for d in (2, 1, 3):
        at_copy(1, d).start()

    @pl.when(last)
    def _():
        at_copy(1, 0).start()

    @pl.when(jnp.logical_not(last))
    def _():
        at_own(1).start()

    e_copy.wait()
    for k in range(NCH):
        rs = pl.ds(k * CH, CH)
        state = s_k[k].astype(F32) + per_head(jnp.exp(offs[k])) * s_in[...].astype(F32)
        carried = jnp.dot(
            u[rs, D + N : D + 2 * N], state.astype(BF), preferred_element_type=F32
        )
        e_k = jnp.exp(la_ref[rs, :])
        for h in range(H):
            hs = slice(h * HP, (h + 1) * HP)
            m = yv[rs, hs] + e_k[:, h : h + 1] * carried[:, hs]
            ssm[rs, hs] = (m * inv_rms(m, 1e-5)).astype(BF)

    loads[4].wait()

    def out_ssm(j, _):
        cs = pl.ds(pl.multiple_of(j * TILE, TILE), TILE)
        part = jnp.dot(ssm[...], wo[:D, cs], preferred_element_type=F32)
        acc[:, :, :, cs] = (part + xv[:, cs].astype(F32)).reshape(4, 2, BLK, TILE)
        return 0

    lax.fori_loop(0, D // TILE, out_ssm, 0)

    out_copies = []
    for par in (1, 0):
        for k in range(4):
            pltpu.make_async_copy(at_send.at[0, pl.ds(0, 64), :], at_recv.at[par, k], at_rsem.at[par, k]).wait()
        if par == 0:

            @pl.when(t == 0)
            def _():
                at_recv[0, 0] = jnp.zeros((BLK, AW), BF)

        def out_att(j, _, par=par):
            cs = pl.ds(pl.multiple_of(j * TILE, TILE), TILE)
            rows = at_recv[par].reshape(4 * BLK, AW)
            part = jnp.dot(rows, wo[D:, cs], preferred_element_type=F32)
            ob[par, :, :, cs] = (part.reshape(4, BLK, TILE) + acc[:, par, :, cs]).astype(BF)
            return 0

        lax.fori_loop(0, D // TILE, out_att, 0)
        for k in range(4):
            cp = pltpu.make_async_copy(
                ob.at[par, k], out_h.at[pl.ds(128 * k + 64 * par, 64), :], load_sem.at[5 + 4 * par + k]
            )
            cp.start()
            out_copies.append(cp)

    for i in range(2):
        for d in (1, 2, 3):
            x_copy(i, d).wait_send()
            at_copy(i, d).wait_send()

    @pl.when(last)
    def _():
        at_copy(1, 0).wait_send()

    q_copy(0).wait_send()
    for k in (1, 2, 3):

        @pl.when(y != k - 1)
        def _(k=k):
            q_copy(k).wait_send()

    for cp in out_copies:
        cp.wait()


def on_device(latents, mixer_weight, step_weight, step_bias, decay_rate, attend_weight, output_weight):
    any_spec = pl.BlockSpec(memory_space=pl.ANY)
    vmem_spec = pl.BlockSpec(memory_space=pltpu.VMEM)
    dma = pltpu.SemaphoreType.DMA
    v = pltpu.VMEM
    scratch = [
        v((ROWS, D), BF),
        v((2, POS, D), BF),
        v((D, D + 2 * N), BF),
        v((D, H), BF),
        v((D, 3 * AW), BF),
        v((D + AW, D), BF),
        v((ROWS, D + 2 * N), BF),
        v((ROWS, D), F32),
        v((4, 2, BLK, D), F32),
        v((2, 4, BLK, D), BF),
        v((ROWS, D), BF),
        v((2, POS, 2 * AW), BF),
        v((2, POS, AW), BF),
        v((4, BLK, AW), BF),
        v((2, POS, AW), BF),
        v((2, 4, BLK, AW), BF),
        v((ROWS, 128), F32),
        v((POS, 128), F32),
        v((ROWS, H), F32),
        v((NCH, H, CH), F32),
        v((NCH, H, CH), F32),
        v((N, D), F32),
        v((NCH, N, D), BF),
        v((N, D), BF),
        v((64, D), BF),
        v((64, D), BF),
        v((4, 16, D), BF),
        v((4, 16, D), F32),
        v((16, D), BF),
        v((4, 16, D), BF),
        v((4, 16, D), BF),
        v((4, 16, D), BF),
        v((64, D), BF),
        v((N, D), BF),
        v((8, 128), F32),
        v((8, 128), F32),
        v((8, 128), F32),
        v((4, 8, 128), F32),
        v((8, 128), F32),
        v((4, 8, 128), F32),
        dma((13,)),
        dma((2,)),
        dma((2, 4)),
        dma((2, 4)),
        dma((4,)),
        dma((4,)),
        dma((2, 4)),
        dma((2, 4)),
        dma((2,)),
        dma((2,)),
        dma((2, 4)),
        dma((2, 4)),
        dma((2, 4)),
        dma((2, 4)),
        dma((4,)),
        dma((4,)),
        dma,
        dma,
    ]
    out = pl.pallas_call(
        kernel,
        out_shape=jax.ShapeDtypeStruct((ROWS, D), BF),
        in_specs=[any_spec, any_spec, any_spec, vmem_spec, vmem_spec, any_spec, any_spec],
        out_specs=any_spec,
        scratch_shapes=scratch,
        compiler_params=pltpu.CompilerParams(
            collective_id=0, has_side_effects=True, vmem_limit_bytes=60 * 2**20
        ),
        cost_estimate=pl.CostEstimate(
            flops=12_000_000_000, bytes_accessed=24_000_000, transcendentals=4_000_000
        ),
    )(
        latents.reshape(ROWS, D),
        mixer_weight,
        step_weight,
        step_bias.reshape(1, H),
        decay_rate.reshape(1, H),
        attend_weight,
        output_weight,
    )
    return out.reshape(FR, BLK, D)


def solution(mesh):
    in_specs = (P("tm", "space", None), P(), P(), P(), P(), P(), P())
    out_specs = P("tm", "space", None)
    return jax.shard_map(
        on_device, mesh=mesh, in_specs=in_specs, out_specs=out_specs, check_vma=False
    )
```

time: 581 us -> 60.8 us (0.10)
  the two profiles are of different devices: /device:TPU:32 before, /device:TPU:1 now
where the time goes in v1:
time: 60.8 us; the launch traced here: 60.5 us
  Pallas kernels  56 us (92%)
  local copies, waits for them, and re-layouts  4.41 us (7%)
    pallas_call x1, Pallas kernels, on_device(): pl.pallas_call(kernel, out_shape=jax.ShapeDtypeStruct((ROWS, D), BF), in_...  56 us
    unnamed x2, local copies, waits for them, and re-layouts  4.41 us

profile of v1, /device:TPU:1, one launch (start us, length us, event | category | flops | bytes accessed | tf_op | source)
XLA Modules:
  0.0 60.5 jit_solution(7219171560547094644)
XLA Ops:
  0.0 1.8 %copy.8.ws_h = bf16[1536,12]{1,0:T(8,128)(2,1)} copy(bf16[1536,12]{0,1:T(8,128)(2,1)} %param.9) | data formatting | bytes 73728 | tf_op args[2]
  1.8 56.0 %shard_map.73 = bf16[512,1536]{1,0:T(8,128)(2,1)} custom-call(bf16[512,1536]{1,0:T(8,128)(2,1)} %bitcast.5, bf16[1536,1792]{1,0:T(8,128)(2,1)} %wm_h.1, bf16[1536,12]{1,0:T(8,128)(2,1)} %copy.8.ws_h, f32[1,12]{1,0:T(1,128)} %bitcast.6, f32[1,12]{1,0:T(1,128)} %bitcast.7, bf16[1536,2304]{1,0:T(8,128)(2,1)} %wa_h.1, bf16[2304,1536]{1,0:T(8,128)(2,1)} %wo_h.1), custom_call_target="tpu_custom_call" | custom-call | flops 12000000000 | bytes 24000000 | tf_op jit(solution)/shard_map/pallas_call | solution.py:552
  57.8 2.7 %copy.10 = bf16[8,64,1536]{2,1,0:T(8,128)(2,1)} copy(bf16[8,64,1536]{2,1,0:T(8,128)(2,1)} %bitcast.4) | data formatting | bytes 3145728

commit v2 on v1

v2 whole, which is shorter than its diff:
```python
import math

import jax
import jax.numpy as jnp
from jax import lax
from jax.experimental import pallas as pl
from jax.experimental.pallas import tpu as pltpu
from jax.sharding import PartitionSpec as P

MESH = pl.DeviceIdType.MESH
BF = jnp.bfloat16
F32 = jnp.float32
EXACT = lax.Precision.HIGHEST

D = 1536
H = 12
HP = 128
N = 128
AH = 6
AW = AH * HP
FR = 8
BLK = 64
ROWS = FR * BLK
POS = 256
CH = 128
NCH = ROWS // CH
TM = 32
MIX_T = 896
Q_T = 768
KV_T = 768
OUT_T = 768
ATT_T = 768


def per_head(cols):
    rows = cols.shape[0]
    return jnp.concatenate(
        [jnp.broadcast_to(cols[:, h : h + 1], (rows, HP)) for h in range(H)], axis=1
    )


def pair(cols, h):
    shape = (cols.shape[0], HP)
    return jnp.concatenate(
        [jnp.broadcast_to(cols[:, i : i + 1], shape) for i in (h, h + 1)], axis=1
    )


def widen(v, width):
    return jnp.concatenate([v] * (width // 128), axis=1)


def inv_rms(x, eps):
    x = x.astype(F32)
    mean = jnp.sum(x * x, axis=-1, keepdims=True) * (1.0 / x.shape[-1])
    return jnp.broadcast_to(lax.rsqrt(mean + eps), (x.shape[0], 128))


def pair_mean():
    row = lax.broadcasted_iota(jnp.int32, (256, 256), 0)
    col = lax.broadcasted_iota(jnp.int32, (256, 256), 1)
    same = lax.div(row, 128) == lax.div(col, 128)
    return jnp.where(same, 1.0 / HP, 0.0).astype(BF)


def head_scaled(v, eps, mean_of):
    parts = []
    for j in range(0, v.shape[1], 256):
        p = v[:, j : j + 256]
        mean = jnp.dot((p * p).astype(BF), mean_of, preferred_element_type=F32)
        parts.append(p * lax.rsqrt(mean + eps))
    return parts[0] if len(parts) == 1 else jnp.concatenate(parts, axis=1)


def kernel(
    lat, wm_h, ws_h, bias_ref, rate_ref, wa_h, wo_h, out_h,
    xv, xt, wm, ws, wa, wo, u, yv, acc, ob, ssm,
    kv, qt, qe, at_send, at_recv,
    r_ref, rt_ref, la_ref, off_ref, lat_t, dt_t,
    s_ref, s_k, l_bf, a_recv, t_bf, b_recv, dec_ref, d_send, d_recv, e_send, s_in,
    ld_own, ld_a, ld_t, ld_b,
    load_sem, own_sem, x_ssem, x_rsem, q_ssem, q_rsem, at_ssem, at_rsem,
    a_ssem, a_rsem, b_ssem, b_rsem, d_ssem, d_rsem, e_ssem, e_rsem, answer_sem, go_sem,
):
    t = lax.axis_index("tm")
    y = lax.axis_index("space")
    core = lax.rem(t, 2)
    x = lax.rem(lax.div(t, 2), 4)
    z = lax.div(t, 8)
    t_next = lax.rem(t + 1, TM)
    t_prev = lax.rem(t + TM - 1, TM)
    ys = [lax.rem(y + d, 4) for d in range(4)]
    mate = (t + 1 - 2 * core, y)
    chip = z * 4 + x
    xs = [lax.rem(x + d, 4) for d in range(4)]
    zs = [lax.rem(z + d, 4) for d in range(4)]
    plane = [(i, j) for i in range(4) for j in range(4) if i + j > 0]

    def chip_dev(i, j):
        return (zs[i] * 8 + xs[j] * 2 + core, y)
    last = y == 3

    def remote(src, dst, ssem, rsem, dev):
        return pltpu.make_async_remote_copy(
            src_ref=src, dst_ref=dst, send_sem=ssem, recv_sem=rsem,
            device_id=dev, device_id_type=MESH,
        )

    loads = [
        pltpu.make_async_copy(src, dst, load_sem.at[i])
        for i, (src, dst) in enumerate([(lat, xv), (ws_h, ws), (wm_h, wm), (wa_h, wa), (wo_h, wo)])
    ]
    for i in (0, 1, 2):
        loads[i].start()

    mean_of = pair_mean()
    barrier = pltpu.get_barrier_semaphore()

    def greet(dev):
        pl.semaphore_signal(barrier, inc=1, device_id=dev, device_id_type=MESH)

    gateway = y == 0
    for d in (1, 2, 3):
        greet((t, ys[d]))

    @pl.when(gateway)
    def _():
        pl.semaphore_wait(answer_sem, 3)
        for i, j in plane:
            greet(chip_dev(i, j))
        greet((t_prev, y))
        greet((t_next, y))

    @pl.when(jnp.logical_not(gateway))
    def _():
        pl.semaphore_wait(barrier, 3)
        pl.semaphore_signal(answer_sem, inc=1, device_id=(t, 0), device_id_type=MESH)

    def x_copy(i, d):
        return remote(
            lat.at[pl.ds(pl.multiple_of(128 * ys[d] + 64 * i, 64), 64), :],
            xt.at[i, pl.ds(pl.multiple_of(64 * y, 64), 64), :],
            x_ssem.at[i, d], x_rsem.at[i, d], (t, ys[d]),
        )

    def x_own(i):
        return pltpu.make_async_copy(
            lat.at[pl.ds(pl.multiple_of(128 * y + 64 * i, 64), 64), :],
            xt.at[i, pl.ds(pl.multiple_of(64 * y, 64), 64), :],
            own_sem.at[i],
        )

    for d in (2, 1, 3):
        x_copy(0, d).start()
    for d in (2, 1, 3):
        x_copy(1, d).start()
    x_own(0).start()
    x_own(1).start()
    loads[3].start()
    loads[4].start()

    loads[0].wait()

    def norm_rows(j, _):
        rs = pl.ds(pl.multiple_of(j * 64, 64), 64)
        r_ref[rs, :] = inv_rms(xv[rs, :], 1e-6)
        return 0

    lax.fori_loop(0, ROWS // 64, norm_rows, 0)
    loads[1].wait()
    loads[2].wait()

    steps = lax.dot_general(
        xv[...], ws[...], (((1,), (1,)), ((), ())), preferred_element_type=F32
    )
    steps = steps * r_ref[:, :H] + bias_ref[...]
    dt = jnp.maximum(steps, 0.0) + jnp.log(1.0 + jnp.exp(-jnp.abs(steps)))
    rate = rate_ref[...]
    row_id = lax.broadcasted_iota(jnp.int32, (CH, CH), 0)
    col_id = lax.broadcasted_iota(jnp.int32, (CH, CH), 1)
    causal = row_id >= col_id
    tri = jnp.where(causal, 1.0, 0.0).astype(F32)
    eye = jnp.where(row_id == col_id, 1.0, 0.0).astype(F32)
    offs = [jnp.zeros((1, H), F32)]
    ends = []
    fe = []
    for k in range(NCH):
        dt_k = dt[k * CH : (k + 1) * CH, :]
        a_k = -rate * dt_k
        la_k = jnp.dot(tri, a_k, precision=EXACT, preferred_element_type=F32)
        la_ref[k * CH : (k + 1) * CH, :] = la_k
        lat_t[k] = lax.dot_general(
            a_k, tri, (((0,), (1,)), ((), ())), precision=EXACT, preferred_element_type=F32
        )
        dt_t[k] = lax.dot_general(
            dt_k, eye, (((0,), (1,)), ((), ())), precision=EXACT, preferred_element_type=F32
        )
        end_k = la_k[CH - 1 : CH, :]
        ends.append(end_k)
        off_ref[k, 0:1, 0:H] = offs[-1]
        offs.append(offs[-1] + end_k)
        fe.append(jnp.exp(end_k - la_k) * dt_k)
    ld_own[...] = jnp.zeros((8, 128), F32)
    ld_t[...] = jnp.zeros((8, 128), F32)
    ld_own[0:1, 0:H] = offs[NCH]

    def mix(j, _):
        cs = pl.ds(pl.multiple_of(j * MIX_T, MIX_T), MIX_T)
        part = jnp.dot(xv[...], wm[:, cs], preferred_element_type=F32)
        u[:, cs] = (part * widen(r_ref[...], MIX_T)).astype(BF)
        return 0

    lax.fori_loop(0, (D + 2 * N) // MIX_T, mix, 0)

    @pl.when(gateway)
    def _():
        pl.semaphore_wait(barrier, 20)
        for d in (1, 2, 3):
            pl.semaphore_signal(go_sem, inc=1, device_id=(t, ys[d]), device_id_type=MESH)

    for k in range(NCH):
        rs = pl.ds(k * CH, CH)
        scaled = (per_head(fe[k]) * u[rs, :D].astype(F32)).astype(BF)
        add = lax.dot_general(
            u[rs, D : D + N], scaled, (((0,), (0,)), ((), ())), preferred_element_type=F32
        )
        if k == 0:
            s_k[0] = jnp.zeros((N, D), BF)
            s_ref[...] = add
        else:
            s_k[k] = s_ref[...].astype(BF)
            s_ref[...] = s_ref[...] * per_head(jnp.exp(ends[k])) + add
    l_bf[...] = s_ref[...].astype(BF)

    loads[3].wait()

    def q_even(j, _):
        cs = pl.ds(pl.multiple_of(j * Q_T, Q_T), Q_T)
        rows = xv[...].reshape(4, 2, BLK, D)[:, 0].reshape(4 * BLK, D)
        scale = r_ref[...].reshape(4, 2, BLK, 128)[:, 0].reshape(4 * BLK, 128)
        part = jnp.dot(rows, wa[:, cs], preferred_element_type=F32) * widen(scale, Q_T)
        qe[:, :, cs] = head_scaled(part, 1e-6, mean_of).astype(BF).reshape(4, BLK, Q_T)
        return 0

    def q_copy(k):
        dev = (t_prev, 3) if k == 0 else (t, k - 1)
        return remote(
            qe.at[k], qt.at[1, pl.ds(pl.multiple_of(64 * y, 64), 64), :],
            q_ssem.at[k], q_rsem.at[y], dev,
        )

    def q_own(k):
        return pltpu.make_async_copy(
            qe.at[k], qt.at[1, pl.ds(pl.multiple_of(64 * y, 64), 64), :], q_rsem.at[y]
        )

    def diag(k, _):
        rs = pl.ds(pl.multiple_of(k * CH, CH), CH)
        cb = lax.dot_general(
            u[rs, D + N : D + 2 * N], u[rs, D : D + N], (((1,), (1,)), ((), ())),
            preferred_element_type=F32,
        )
        la_k = la_ref[rs, :]
        la_row = lat_t[k]
        dt_row = dt_t[k]
        for h in range(H):
            gap = la_k[:, h : h + 1] - la_row[h : h + 1, :]
            w = jnp.exp(jnp.where(causal, gap, -1e30)) * cb * dt_row[h : h + 1, :]
            yv[rs, h * HP : (h + 1) * HP] = jnp.dot(
                w.astype(BF), u[rs, h * HP : (h + 1) * HP], preferred_element_type=F32
            )
        return 0


    def attend_proj(i, width_from, dst, dst_from, tiles, scaled_tiles):
        def body(j, _):
            src = pl.ds(pl.multiple_of(width_from + j * KV_T, KV_T), KV_T)
            to = pl.ds(pl.multiple_of(dst_from + j * KV_T, KV_T), KV_T)
            part = jnp.dot(xt[i], wa[:, src], preferred_element_type=F32)
            part = part * widen(rt_ref[...], KV_T)
            if scaled_tiles:
                part = head_scaled(part, 1e-6, mean_of)
            dst[i, :, to] = part.astype(BF)
            return 0

        lax.fori_loop(0, tiles, body, 0)

    def norm_frame(i):
        def body(j, _):
            rs = pl.ds(pl.multiple_of(j * 64, 64), 64)
            rt_ref[rs, :] = inv_rms(xt[i, rs, :], 1e-6)
            return 0

        lax.fori_loop(0, POS // 64, body, 0)

    def frame_arrived(i):
        for d in (1, 2, 3):
            x_copy(i, d).wait_recv()
        x_own(i).wait()

    half = pl.ds(pl.multiple_of(64 * core, 64), 64)
    other_half = pl.ds(pl.multiple_of(64 - 64 * core, 64), 64)
    a_copy = remote(l_bf.at[other_half, :], a_recv, a_ssem.at[0], a_rsem.at[0], mate)
    ld_copy = remote(ld_own, ld_a, a_ssem.at[1], a_rsem.at[1], mate)

    @pl.when(jnp.logical_not(gateway))
    def _():
        pl.semaphore_wait(go_sem, 1)

    ld_copy.start()
    a_copy.start()

    for d in (1, 2, 3):
        x_copy(0, d).wait_send()


    lax.fori_loop(0, 2, diag, 0)

    a_copy.wait()
    ld_copy.wait()
    first = core == 0
    ld_mine = ld_own[0:1, 0:H]
    ld_theirs = ld_a[0:1, 0:H]
    ld0 = jnp.where(first, ld_mine, ld_theirs)
    ld1 = jnp.where(first, ld_theirs, ld_mine)
    ld_t[0:1, 0:H] = ld0 + ld1
    ld_b[chip] = ld_t[...]
    ld_copies = [remote(ld_t, ld_b.at[chip], b_ssem.at[1], b_rsem.at[1], chip_dev(i, j)) for i, j in plane]
    for cp in ld_copies:
        cp.start()

    mine = s_ref[half, :]
    theirs = a_recv[...].astype(F32)
    l0 = jnp.where(first, mine, theirs)
    l1 = jnp.where(first, theirs, mine)
    t_bf[...] = (per_head(jnp.exp(ld1)) * l0 + l1).astype(BF)

    def piece(ref, i, j):
        rows = pl.ds(pl.multiple_of(16 * j, 16), 16)
        lanes = pl.ds(pl.multiple_of(384 * i, 128), 384)
        return ref.at[rows, lanes]

    b_recv[chip] = t_bf[pl.ds(pl.multiple_of(16 * x, 16), 16), pl.ds(pl.multiple_of(384 * z, 128), 384)]
    for i, j in plane:
        remote(piece(t_bf, zs[i], xs[j]), b_recv.at[chip], b_ssem.at[0], b_rsem.at[0], chip_dev(i, j)).start()

    lax.fori_loop(0, AW // Q_T, q_even, 0)

    q_copy(0).start()
    for k in (1, 2, 3):

        @pl.when(y != k - 1)
        def _(k=k):
            q_copy(k).start()

        @pl.when(y == k - 1)
        def _(k=k):
            q_own(k).start()

    lax.fori_loop(2, 4, diag, 0)
    frame_arrived(0)
    norm_frame(0)
    attend_proj(0, AW, kv, 0, AW // KV_T, True)

    attend_proj(0, 2 * AW, kv, AW, AW // KV_T, False)

    def all_arrived(buf, ssem, rsem):
        part = buf.at[pl.ds(0, 15)]
        pltpu.make_async_copy(part, part, ssem).wait()
        pltpu.make_async_copy(part, part, rsem).wait()

    all_arrived(ld_b, b_ssem.at[1], b_rsem.at[1])
    all_arrived(b_recv, b_ssem.at[0], b_rsem.at[0])
    dec_ref[...] = per_head(jnp.exp(ld_b[:, 0, 0:H]))
    own_lanes = pl.ds(pl.multiple_of(384 * z, 128), 384)
    run = jnp.zeros((16, 384), F32)
    for j in range(16):
        d_send[j] = run.astype(BF)
        run = run * dec_ref[j : j + 1, own_lanes] + b_recv[j].astype(F32)
    own_rows = pl.ds(pl.multiple_of(16 * x, 16), 16)
    d_recv[own_rows, own_lanes] = d_send[chip]
    for i, j in plane:
        remote(
            d_send.at[zs[i] * 4 + xs[j]], piece(d_recv, z, x), d_ssem, d_rsem, chip_dev(i, j)
        ).start()

    frame_arrived(1)
    for d in (1, 2, 3):
        x_copy(1, d).wait_send()
    norm_frame(1)


    def q_odd(j, _):
        cs = pl.ds(pl.multiple_of(j * Q_T, Q_T), Q_T)
        part = jnp.dot(xt[1], wa[:, cs], preferred_element_type=F32) * widen(rt_ref[...], Q_T)
        qt[0, :, cs] = head_scaled(part, 1e-6, mean_of).astype(BF)
        return 0

    lax.fori_loop(0, AW // Q_T, q_odd, 0)

    def attention(i):
        for h in range(AH):
            hs = slice(h * HP, (h + 1) * HP)
            vs = slice(AW + h * HP, AW + (h + 1) * HP)
            s = lax.dot_general(
                qt[i, :, hs], kv[i, :, hs], (((1,), (1,)), ((), ())), preferred_element_type=F32
            )
            p = jnp.exp(s * (1.0 / math.sqrt(HP)))
            total = jnp.sum(p, axis=-1, keepdims=True)
            num = jnp.dot(p.astype(BF), kv[i, :, vs], preferred_element_type=F32)
            at_send[i, :, hs] = (num / total).astype(BF)

    def at_copy(i, d):
        src = at_send.at[i, pl.ds(pl.multiple_of(64 * ys[d], 64), 64), :]
        if i == 0:
            return remote(src, at_recv.at[1, y], at_ssem.at[i, d], at_rsem.at[1, y], (t, ys[d]))
        owner = jnp.where(last, t_next, t)
        k = ys[1]
        return remote(src, at_recv.at[0, k], at_ssem.at[i, d], at_rsem.at[0, k], (owner, ys[d]))

    def at_own(i):
        src = at_send.at[i, pl.ds(pl.multiple_of(64 * y, 64), 64), :]
        if i == 0:
            return pltpu.make_async_copy(src, at_recv.at[1, y], at_rsem.at[1, y])
        return pltpu.make_async_copy(src, at_recv.at[0, ys[1]], at_rsem.at[0, ys[1]])

    attention(0)
    for d in (2, 1, 3):
        at_copy(0, d).start()
    at_own(0).start()

    attend_proj(1, AW, kv, 0, AW // KV_T, True)
    attend_proj(1, 2 * AW, kv, AW, AW // KV_T, False)
    all_arrived(d_send, d_ssem, d_rsem)
    inc0 = d_recv[...].astype(F32)
    inc1 = per_head(jnp.exp(ld0)) * inc0 + l0
    e_send[...] = jnp.where(first, inc1, inc0).astype(BF)
    s_in[half, :] = jnp.where(first, inc0, inc1).astype(BF)
    e_copy = remote(e_send, s_in.at[half, :], e_ssem, e_rsem, mate)
    e_copy.start()

    for k in range(4):
        pltpu.make_async_copy(qe.at[k], qt.at[1, pl.ds(64 * k, 64), :], q_rsem.at[k]).wait()
    attention(1)
    for d in (2, 1, 3):
        at_copy(1, d).start()

    @pl.when(last)
    def _():
        at_copy(1, 0).start()

    @pl.when(jnp.logical_not(last))
    def _():
        at_own(1).start()

    e_copy.wait()


    def mixed(k, _):
        rs = pl.ds(pl.multiple_of(k * CH, CH), CH)
        c_k = u[rs, D + N : D + 2 * N]
        e_k = jnp.exp(la_ref[rs, :])
        e_in = jnp.exp(off_ref[k][0:1, 0:H])
        for h in range(0, H, 2):
            hs = slice(h * HP, (h + 2) * HP)
            state = s_k[k, :, hs].astype(F32) + pair(e_in, h) * s_in[:, hs].astype(F32)
            carried = jnp.dot(c_k, state.astype(BF), preferred_element_type=F32)
            m = yv[rs, hs] + pair(e_k, h) * carried
            ssm[rs, hs] = head_scaled(m, 1e-5, mean_of).astype(BF)
        return 0

    lax.fori_loop(0, NCH, mixed, 0)

    loads[4].wait()

    def out_ssm(j, _):
        cs = pl.ds(pl.multiple_of(j * OUT_T, OUT_T), OUT_T)
        part = jnp.dot(ssm[...], wo[:D, cs], preferred_element_type=F32)
        acc[:, :, :, cs] = (part + xv[:, cs].astype(F32)).reshape(4, 2, BLK, OUT_T)
        return 0

    lax.fori_loop(0, D // OUT_T, out_ssm, 0)

    out_copies = []
    for par in (1, 0):
        for k in range(4):
            pltpu.make_async_copy(at_send.at[0, pl.ds(0, 64), :], at_recv.at[par, k], at_rsem.at[par, k]).wait()
        if par == 0:

            @pl.when(t == 0)
            def _():
                at_recv[0, 0] = jnp.zeros((BLK, AW), BF)

        def out_att(j, _, par=par):
            cs = pl.ds(pl.multiple_of(j * ATT_T, ATT_T), ATT_T)
            rows = at_recv[par].reshape(4 * BLK, AW)
            part = jnp.dot(rows, wo[D:, cs], preferred_element_type=F32)
            ob[par, :, :, cs] = (part.reshape(4, BLK, ATT_T) + acc[:, par, :, cs]).astype(BF)
            return 0

        lax.fori_loop(0, D // ATT_T, out_att, 0)
        for k in range(4):
            cp = pltpu.make_async_copy(
                ob.at[par, k], out_h.at[pl.ds(128 * k + 64 * par, 64), :], load_sem.at[5 + 4 * par + k]
            )
            cp.start()
            out_copies.append(cp)

    for i in range(2):
        for d in (1, 2, 3):
            at_copy(i, d).wait_send()

    @pl.when(last)
    def _():
        at_copy(1, 0).wait_send()

    q_copy(0).wait_send()
    for k in (1, 2, 3):

        @pl.when(y != k - 1)
        def _(k=k):
            q_copy(k).wait_send()

    for cp in out_copies:
        cp.wait()


def on_device(latents, mixer_weight, step_weight, step_bias, decay_rate, attend_weight, output_weight):
    any_spec = pl.BlockSpec(memory_space=pl.ANY)
    vmem_spec = pl.BlockSpec(memory_space=pltpu.VMEM)
    dma = pltpu.SemaphoreType.DMA
    v = pltpu.VMEM
    scratch = [
        v((ROWS, D), BF),
        v((2, POS, D), BF),
        v((D, D + 2 * N), BF),
        v((H, D), BF),
        v((D, 3 * AW), BF),
        v((D + AW, D), BF),
        v((ROWS, D + 2 * N), BF),
        v((ROWS, D), F32),
        v((4, 2, BLK, D), F32),
        v((2, 4, BLK, D), BF),
        v((ROWS, D), BF),
        v((2, POS, 2 * AW), BF),
        v((2, POS, AW), BF),
        v((4, BLK, AW), BF),
        v((2, POS, AW), BF),
        v((2, 4, BLK, AW), BF),
        v((ROWS, 128), F32),
        v((POS, 128), F32),
        v((ROWS, H), F32),
        v((NCH, 8, 128), F32),
        v((NCH, H, CH), F32),
        v((NCH, H, CH), F32),
        v((N, D), F32),
        v((NCH, N, D), BF),
        v((N, D), BF),
        v((64, D), BF),
        v((64, D), BF),
        v((16, 16, 384), BF),
        v((16, D), F32),
        v((16, 16, 384), BF),
        v((64, D), BF),
        v((64, D), BF),
        v((N, D), BF),
        v((8, 128), F32),
        v((8, 128), F32),
        v((8, 128), F32),
        v((16, 8, 128), F32),
        dma((13,)),
        dma((2,)),
        dma((2, 4)),
        dma((2, 4)),
        dma((4,)),
        dma((4,)),
        dma((2, 4)),
        dma((2, 4)),
        dma((2,)),
        dma((2,)),
        dma((2,)),
        dma((2,)),
        dma,
        dma,
        dma,
        dma,
        pltpu.SemaphoreType.REGULAR,
        pltpu.SemaphoreType.REGULAR,
    ]
    out = pl.pallas_call(
        kernel,
        out_shape=jax.ShapeDtypeStruct((ROWS, D), BF),
        in_specs=[any_spec, any_spec, any_spec, vmem_spec, vmem_spec, any_spec, any_spec],
        out_specs=any_spec,
        scratch_shapes=scratch,
        compiler_params=pltpu.CompilerParams(
            collective_id=0, has_side_effects=True, vmem_limit_bytes=60 * 2**20
        ),
        cost_estimate=pl.CostEstimate(
            flops=12_000_000_000, bytes_accessed=24_000_000, transcendentals=4_000_000
        ),
    )(
        latents.reshape(ROWS, D),
        mixer_weight,
        step_weight.T,
        step_bias.reshape(1, H),
        decay_rate.reshape(1, H),
        attend_weight,
        output_weight,
    )
    return out.reshape(FR, BLK, D)


def solution(mesh):
    in_specs = (P("tm", "space", None), P(), P(), P(), P(), P(), P())
    out_specs = P("tm", "space", None)
    return jax.shard_map(
        on_device, mesh=mesh, in_specs=in_specs, out_specs=out_specs, check_vma=False
    )
```

time: 60.8 us -> 47 us (0.77)
  the two profiles are of different devices: /device:TPU:1 before, /device:TPU:0 now
where the time goes in v2:
time: 47 us; the launch traced here: 46.8 us
  Pallas kernels  44.2 us (94%)
  local copies, waits for them, and re-layouts  2.65 us (6%)
    pallas_call x1, Pallas kernels, on_device(): pl.pallas_call(kernel, out_shape=jax.ShapeDtypeStruct((ROWS, D), BF), in_...  44.2 us
    unnamed x1, local copies, waits for them, and re-layouts  2.65 us

profile of v2, /device:TPU:0, one launch (start us, length us, event | category | flops | bytes accessed | tf_op | source)
XLA Modules:
  0.0 46.8 jit_solution(698585807586948642)
XLA Ops:
  0.0 44.2 %shard_map.73 = bf16[512,1536]{1,0:T(8,128)(2,1)} custom-call(bf16[512,1536]{1,0:T(8,128)(2,1)} %bitcast.6, bf16[1536,1792]{1,0:T(8,128)(2,1)} %wm_h.1, bf16[12,1536]{1,0:T(8,128)(2,1)} %bitcast.7, f32[1,12]{1,0:T(1,128)} %bitcast.8, f32[1,12]{1,0:T(1,128)} %bitcast.9, bf16[1536,2304]{1,0:T(8,128)(2,1)} %wa_h.1, bf16[2304,1536]{1,0:T(8,128)(2,1)} %wo_h.1), custom_call_target="tpu_custom_call" | custom-call | flops 12000000000 | bytes 24000000 | tf_op jit(solution)/shard_map/pallas_call | solution.py:590
  44.2 2.7 %copy.9 = bf16[8,64,1536]{2,1,0:T(8,128)(2,1)} copy(bf16[8,64,1536]{2,1,0:T(8,128)(2,1)} %bitcast.5) | data formatting | bytes 3145728

commit v3 on v2

--- a/solution.py
+++ b/solution.py
@@ -28,8 +28,8 @@
 MIX_T = 896
 Q_T = 768
 KV_T = 768
-OUT_T = 768
-ATT_T = 768
+OUT_T = 1536
+ATT_T = 1536
 
 
 def per_head(cols):
@@ -73,8 +73,8 @@
 
 
 def kernel(
-    lat, wm_h, ws_h, bias_ref, rate_ref, wa_h, wo_h, out_h,
-    xv, xt, wm, ws, wa, wo, u, yv, acc, ob, ssm,
+    lat, wm_h, ws_h, bias_ref, rate_ref, wa_h, wo_h, out_ref,
+    xv, xt, wm, ws, wa, wo, u, yv, acc, ssm,
     kv, qt, qe, at_send, at_recv,
     r_ref, rt_ref, la_ref, off_ref, lat_t, dt_t,
     s_ref, s_k, l_bf, a_recv, t_bf, b_recv, dec_ref, d_send, d_recv, e_send, s_in,
@@ -99,6 +99,7 @@
     def chip_dev(i, j):
         return (zs[i] * 8 + xs[j] * 2 + core, y)
     last = y == 3
+    followed = jnp.logical_or(t < TM - 1, y < 3)
 
     def remote(src, dst, ssem, rsem, dev):
         return pltpu.make_async_remote_copy(
@@ -189,12 +190,6 @@
         a_k = -rate * dt_k
         la_k = jnp.dot(tri, a_k, precision=EXACT, preferred_element_type=F32)
         la_ref[k * CH : (k + 1) * CH, :] = la_k
-        lat_t[k] = lax.dot_general(
-            a_k, tri, (((0,), (1,)), ((), ())), precision=EXACT, preferred_element_type=F32
-        )
-        dt_t[k] = lax.dot_general(
-            dt_k, eye, (((0,), (1,)), ((), ())), precision=EXACT, preferred_element_type=F32
-        )
         end_k = la_k[CH - 1 : CH, :]
         ends.append(end_k)
         off_ref[k, 0:1, 0:H] = offs[-1]
@@ -310,11 +305,16 @@
     ld_copy.start()
     a_copy.start()
 
-    for d in (1, 2, 3):
-        x_copy(0, d).wait_send()
-
-
-    lax.fori_loop(0, 2, diag, 0)
+    for k in range(NCH):
+        dt_k = dt[k * CH : (k + 1) * CH, :]
+        a_k = -rate * dt_k
+        lat_t[k] = lax.dot_general(
+            a_k, tri, (((0,), (1,)), ((), ())), precision=EXACT, preferred_element_type=F32
+        )
+        dt_t[k] = lax.dot_general(
+            dt_k, eye, (((0,), (1,)), ((), ())), precision=EXACT, preferred_element_type=F32
+        )
+
 
     a_copy.wait()
     ld_copy.wait()
@@ -346,7 +346,10 @@
 
     lax.fori_loop(0, AW // Q_T, q_even, 0)
 
-    q_copy(0).start()
+    @pl.when(t > 0)
+    def _():
+        q_copy(0).start()
+
     for k in (1, 2, 3):
 
         @pl.when(y != k - 1)
@@ -357,7 +360,7 @@
         def _(k=k):
             q_own(k).start()
 
-    lax.fori_loop(2, 4, diag, 0)
+    lax.fori_loop(0, 4, diag, 0)
     frame_arrived(0)
     norm_frame(0)
     attend_proj(0, AW, kv, 0, AW // KV_T, True)
@@ -385,8 +388,6 @@
         ).start()
 
     frame_arrived(1)
-    for d in (1, 2, 3):
-        x_copy(1, d).wait_send()
     norm_frame(1)
 
 
@@ -439,13 +440,15 @@
     e_copy = remote(e_send, s_in.at[half, :], e_ssem, e_rsem, mate)
     e_copy.start()
 
-    for k in range(4):
-        pltpu.make_async_copy(qe.at[k], qt.at[1, pl.ds(64 * k, 64), :], q_rsem.at[k]).wait()
-    attention(1)
-    for d in (2, 1, 3):
-        at_copy(1, d).start()
-
-    @pl.when(last)
+    @pl.when(followed)
+    def _():
+        for k in range(4):
+            pltpu.make_async_copy(qe.at[k], qt.at[1, pl.ds(64 * k, 64), :], q_rsem.at[k]).wait()
+        attention(1)
+        for d in (2, 1, 3):
+            at_copy(1, d).start()
+
+    @pl.when(jnp.logical_and(last, followed))
     def _():
         at_copy(1, 0).start()
 
@@ -481,11 +484,18 @@
 
     lax.fori_loop(0, D // OUT_T, out_ssm, 0)
 
-    out_copies = []
     for par in (1, 0):
         for k in range(4):
-            pltpu.make_async_copy(at_send.at[0, pl.ds(0, 64), :], at_recv.at[par, k], at_rsem.at[par, k]).wait()
-        if par == 0:
+            arrival = pltpu.make_async_copy(
+                at_send.at[0, pl.ds(0, 64), :], at_recv.at[par, k], at_rsem.at[par, k]
+            )
+            if par == 1 or k > 0:
+                arrival.wait()
+                continue
+
+            @pl.when(t > 0)
+            def _(arrival=arrival):
+                arrival.wait()
 
             @pl.when(t == 0)
             def _():
@@ -495,34 +505,35 @@
             cs = pl.ds(pl.multiple_of(j * ATT_T, ATT_T), ATT_T)
             rows = at_recv[par].reshape(4 * BLK, AW)
             part = jnp.dot(rows, wo[D:, cs], preferred_element_type=F32)
-            ob[par, :, :, cs] = (part.reshape(4, BLK, ATT_T) + acc[:, par, :, cs]).astype(BF)
+            out_ref[:, par, :, cs] = (part.reshape(4, BLK, ATT_T) + acc[:, par, :, cs]).astype(BF)
             return 0
 
         lax.fori_loop(0, D // ATT_T, out_att, 0)
-        for k in range(4):
-            cp = pltpu.make_async_copy(
-                ob.at[par, k], out_h.at[pl.ds(128 * k + 64 * par, 64), :], load_sem.at[5 + 4 * par + k]
-            )
-            cp.start()
-            out_copies.append(cp)
 
     for i in range(2):
         for d in (1, 2, 3):
-            at_copy(i, d).wait_send()
-
-    @pl.when(last)
+            x_copy(i, d).wait_send()
+    for d in (1, 2, 3):
+        at_copy(0, d).wait_send()
+
+    @pl.when(followed)
+    def _():
+        for d in (1, 2, 3):
+            at_copy(1, d).wait_send()
+
+    @pl.when(jnp.logical_and(last, followed))
     def _():
         at_copy(1, 0).wait_send()
 
-    q_copy(0).wait_send()
+    @pl.when(t > 0)
+    def _():
+        q_copy(0).wait_send()
+
     for k in (1, 2, 3):
 
         @pl.when(y != k - 1)
         def _(k=k):
             q_copy(k).wait_send()
-
-    for cp in out_copies:
-        cp.wait()
 
 
 def on_device(latents, mixer_weight, step_weight, step_bias, decay_rate, attend_weight, output_weight):
@@ -540,7 +551,6 @@
         v((ROWS, D + 2 * N), BF),
         v((ROWS, D), F32),
         v((4, 2, BLK, D), F32),
-        v((2, 4, BLK, D), BF),
         v((ROWS, D), BF),
         v((2, POS, 2 * AW), BF),
         v((2, POS, AW), BF),
@@ -589,9 +599,9 @@
     ]
     out = pl.pallas_call(
         kernel,
-        out_shape=jax.ShapeDtypeStruct((ROWS, D), BF),
+        out_shape=pltpu.VMEM((4, 2, BLK, D), BF),
         in_specs=[any_spec, any_spec, any_spec, vmem_spec, vmem_spec, any_spec, any_spec],
-        out_specs=any_spec,
+        out_specs=vmem_spec,
         scratch_shapes=scratch,
         compiler_params=pltpu.CompilerParams(
             collective_id=0, has_side_effects=True, vmem_limit_bytes=60 * 2**20

time: 47 us -> 41.3 us (0.88)
  the two profiles are of different devices: /device:TPU:0 before, /device:TPU:1 now
where the time goes in v3:
time: 41.3 us; the launch traced here: 41.2 us
  Pallas kernels  40 us (97%)
  local copies, waits for them, and re-layouts  1.15 us (3%)
    pallas_call x1, Pallas kernels, on_device(): pl.pallas_call(kernel, out_shape=pltpu.VMEM((4, 2, BLK, D), BF), in_specs...  40 us
    unnamed x1, local copies, waits for them, and re-layouts  1.15 us

profile of v3, /device:TPU:1, one launch (start us, length us, event | category | flops | bytes accessed | tf_op | source)
XLA Modules:
  0.0 41.2 jit_solution(7263320276616863782)
XLA Ops:
  0.0 40.0 %shard_map.73 = bf16[4,2,64,1536]{3,2,1,0:T(8,128)(2,1)S(1)} custom-call(bf16[512,1536]{1,0:T(8,128)(2,1)} %bitcast.6, bf16[1536,1792]{1,0:T(8,128)(2,1)} %wm_h.1, bf16[12,1536]{1,0:T(8,128)(2,1)} %bitcast.7, f32[1,12]{1,0:T(1,128)} %bitcast.8, f32[1,12]{1,0:T(1,128)} %bitcast.9, bf16[1536,2304]{1,0:T(8,128)(2,1)} %wa_h.1, bf16[2304,1536]{1,0:T(8,128)(2,1)} %wo_h.1), custom_call_target="tpu_custom_call" | custom-call | flops 12000000000 | bytes 24000000 | tf_op jit(solution)/shard_map/pallas_call | solution.py:600
  40.0 1.1 %copy.9 = bf16[8,64,1536]{2,1,0:T(8,128)(2,1)} copy(bf16[8,64,1536]{2,1,0:T(8,128)(2,1)S(1)} %bitcast.5) | data formatting | bytes 3145728

commit v4 on v3

--- a/solution.py
+++ b/solution.py
@@ -280,18 +280,14 @@
 
         lax.fori_loop(0, tiles, body, 0)
 
-    def norm_frame(i):
-        def body(j, _):
-            rs = pl.ds(pl.multiple_of(j * 64, 64), 64)
+    def norm_arriving(i):
+        for d in (0, 1, 3, 2):
+            if d == 0:
+                x_own(i).wait()
+            else:
+                x_copy(i, d).wait_recv()
+            rs = pl.ds(pl.multiple_of(64 * ys[(4 - d) % 4], 64), 64)
             rt_ref[rs, :] = inv_rms(xt[i, rs, :], 1e-6)
-            return 0
-
-        lax.fori_loop(0, POS // 64, body, 0)
-
-    def frame_arrived(i):
-        for d in (1, 2, 3):
-            x_copy(i, d).wait_recv()
-        x_own(i).wait()
 
     half = pl.ds(pl.multiple_of(64 * core, 64), 64)
     other_half = pl.ds(pl.multiple_of(64 - 64 * core, 64), 64)
@@ -361,8 +357,7 @@
             q_own(k).start()
 
     lax.fori_loop(0, 4, diag, 0)
-    frame_arrived(0)
-    norm_frame(0)
+    norm_arriving(0)
     attend_proj(0, AW, kv, 0, AW // KV_T, True)
 
     attend_proj(0, 2 * AW, kv, AW, AW // KV_T, False)
@@ -387,8 +382,7 @@
             d_send.at[zs[i] * 4 + xs[j]], piece(d_recv, z, x), d_ssem, d_rsem, chip_dev(i, j)
         ).start()
 
-    frame_arrived(1)
-    norm_frame(1)
+    norm_arriving(1)
 
 
     def q_odd(j, _):

time: 41.3 us -> 41.1 us (level)
  no operation moved by 1% of the time
where the time goes in v4:
time: 41.1 us; the launch traced here: 41 us
  Pallas kernels  39.8 us (97%)
  local copies, waits for them, and re-layouts  1.15 us (3%)
    pallas_call x1, Pallas kernels, on_device(): pl.pallas_call(kernel, out_shape=pltpu.VMEM((4, 2, BLK, D), BF), in_specs...  39.8 us
    unnamed x1, local copies, waits for them, and re-layouts  1.15 us

profile of v4, /device:TPU:1, one launch (start us, length us, event | category | flops | bytes accessed | tf_op | source)
XLA Modules:
  0.0 41.0 jit_solution(843769185811268382)
XLA Ops:
  0.0 39.8 %shard_map.73 = bf16[4,2,64,1536]{3,2,1,0:T(8,128)(2,1)S(1)} custom-call(bf16[512,1536]{1,0:T(8,128)(2,1)} %bitcast.6, bf16[1536,1792]{1,0:T(8,128)(2,1)} %wm_h.1, bf16[12,1536]{1,0:T(8,128)(2,1)} %bitcast.7, f32[1,12]{1,0:T(1,128)} %bitcast.8, f32[1,12]{1,0:T(1,128)} %bitcast.9, bf16[1536,2304]{1,0:T(8,128)(2,1)} %wa_h.1, bf16[2304,1536]{1,0:T(8,128)(2,1)} %wo_h.1), custom_call_target="tpu_custom_call" | custom-call | flops 12000000000 | bytes 24000000 | tf_op jit(solution)/shard_map/pallas_call | solution.py:594
  39.8 1.1 %copy.9 = bf16[8,64,1536]{2,1,0:T(8,128)(2,1)} copy(bf16[8,64,1536]{2,1,0:T(8,128)(2,1)S(1)} %bitcast.5) | data formatting | bytes 3145728
